TPU v7x, 128 devices: a whole 4x4x4 slice. The times are simulated.
128 devices in a mesh: section: 8 (over x, core), ctx: 16 (over y, z).
Axes of the slice: x: 4, y: 4, z: 4, core: 2. Of those that a mesh axis runs over, the one named last changes fastest.
Arguments:
- tokens: bfloat16 [24576, 8192], P(('section', 'ctx')), may hold values from -60 to 60
- norm_gain: float32 [1, 2, 8192], replicated, may hold values from 0.1 to 1.9
- feat_taps: float32 [1, 2, 3, 3, 8192], replicated, may hold values from -3.5 to 3.5
- se_taps: float32 [1, 7, 8192], replicated, may hold values from -2 to 2
- mr_taps: bfloat16 [1, 128, 512], replicated, may hold values from -0.5 to 0.5
Outputs:
- final: bfloat16 [24576, 8192], P(('section', 'ctx'))
All inputs are finite; a program needn't handle non-finite values.
Results may differ from a plain program's by a relative error of at most 0.0089.
Values may be sent and summed in bfloat16 or wider, within the bound.
No kernel may reach another device: no remote copies, remote signals or barrier semaphores. Data moves between devices by JAX's collectives and lax.ppermute only.
A program may use at most 192 MiB of HBM per device.

v0:
```python
import jax
import jax.numpy as jnp
from jax import lax
from jax.sharding import PartitionSpec as P


def from_behind(x, axis, by):
    length = lax.axis_size(axis)
    pairs = [(i, i + by) for i in range(length) if 0 <= i + by < length]
    return lax.ppermute(x, axis, pairs)


def normalize(rows_in, gain):
    values = rows_in.astype(jnp.float32)
    mean_square = jnp.mean(values * values, axis=-1, keepdims=True)
    return values * lax.rsqrt(mean_square + 1e-06) * gain


def short_filter(product, filter_taps):
    row_total = product.shape[0]
    reach_rows = filter_taps.shape[0] - 1
    summed = filter_taps[0] * product[reach_rows:].astype(jnp.float32)
    for i in range(1, filter_taps.shape[0]):
        summed = summed + filter_taps[i] * product[reach_rows - i : row_total - i].astype(
            jnp.float32
        )
    return summed


def build_table(filter_taps):
    tap_count = filter_taps.shape[0]
    row_index = jnp.arange(64)[:, None]
    col_index = jnp.arange(64 + tap_count - 1)[None, :]
    lag_index = row_index + tap_count - 1 - col_index
    inside = (lag_index >= 0) & (lag_index < tap_count)
    picked = jnp.take(filter_taps.T, jnp.clip(lag_index, 0, tap_count - 1), axis=1)
    return jnp.where(inside[None], picked, jnp.zeros((), filter_taps.dtype))


def long_filter(product, long_table):
    row_total = product.shape[0]
    group_count = long_table.shape[0]
    span_rows = long_table.shape[2]
    out_rows = row_total - (span_rows - 64)
    grouped = product.reshape(row_total, group_count, -1)

    def block_out(block_index):
        window_rows = lax.dynamic_slice_in_dim(grouped, block_index * 64, span_rows, 0)
        return jnp.einsum(
            "gij,jgc->igc", long_table, window_rows, preferred_element_type=jnp.float32
        )

    stacked = lax.map(block_out, jnp.arange(out_rows // 64))
    return stacked.reshape(out_rows, product.shape[1])


def apply_operator(extended, gain, feature_taps, filter_fn, reach_rows):
    scaled = normalize(extended, gain)
    row_total = extended.shape[0]
    lead_rows = feature_taps.shape[1] - 1
    streams = []
    for j in range(3):
        summed = feature_taps[j, 0] * scaled[lead_rows:]
        for i in range(1, feature_taps.shape[1]):
            summed = summed + feature_taps[j, i] * scaled[lead_rows - i : row_total - i]
        streams.append(summed)
    product = (streams[1] * streams[2]).astype(jnp.bfloat16)
    filtered = filter_fn(product)
    gate_rows = streams[0][reach_rows:]
    residual = extended[lead_rows + reach_rows :].astype(jnp.float32)
    return (residual + gate_rows * filtered).astype(jnp.bfloat16)


def on_device(tokens, norm_gain, feat_taps, se_taps, mr_taps):
    lead_rows = feat_taps.shape[3] - 1
    short_reach = se_taps.shape[1] - 1
    long_reach = mr_taps.shape[1] - 1
    rim_short = lead_rows + short_reach
    rim_long = lead_rows + long_reach
    gain_pair = norm_gain[0]
    feature_pair = feat_taps[0]
    short_taps = se_taps[0]
    long_table = build_table(mr_taps[0])
    before = from_behind(tokens[-rim_short:], ("section", "ctx"), 1)
    first_out = apply_operator(
        jnp.concatenate([before, tokens], axis=0),
        gain_pair[0],
        feature_pair[0],
        lambda p: short_filter(p, short_taps),
        short_reach,
    )
    tail_rows = from_behind(first_out[-rim_long:], ("section", "ctx"), 1)
    return apply_operator(
        jnp.concatenate([tail_rows, first_out], axis=0),
        gain_pair[1],
        feature_pair[1],
        lambda p: long_filter(p, long_table),
        long_reach,
    )


def solution(mesh):
    placed = (P(("section", "ctx"), None), P(), P(), P(), P())
    return jax.shard_map(
        on_device,
        mesh=mesh,
        in_specs=placed,
        out_specs=P(("section", "ctx"), None),
        check_vma=False,
    )
```

profile of v0, /device:TPU:7, one launch (start us, length us, event | category | flops | bytes accessed | tf_op | source)
XLA Modules:
  0.0 646.5 jit_solution(11343863659115443276)
XLA Ops:
  4.5 5.9 copy.15
  15.3 50.1 %gather_fusion = bf16[12224,512]{1,0:T(8,128)(2,1)} fusion(bf16[512,128]{0,1:T(8,128)(2,1)S(1)} %bitcast.54, s32[12288]{0:T(1024)S(1)} %pad_clamp_fusion), kind=kCustom, calls=%fused_computation | custom fusion | bytes 25083648 | tf_op jit(solution)/shard_map/jit(_take)/gather | solution.py:36
  65.5 12.5 %reshape.159 = bf16[64,191,512]{2,1,0:T(8,128)(2,1)} reshape(bf16[12224,512]{1,0:T(8,128)(2,1)} %gather_fusion) | data formatting | bytes 25034752 | tf_op jit(solution)/shard_map/jit(_take)/gather | solution.py:36
  79.8 4.9 fusion.5
  84.7 5.7 fusion.6
  90.4 15.7 %multiply_convert_fusion.1 = (bf16[198,8192]{0,1:T(8,128)(2,1)S(1)}, f32[198,8192]{0,1:T(8,128)}, f32[198,8192]{0,1:T(8,128)}, f32[198,8192]{0,1:T(8,128)}) fusion(f32[8192]{0:T(1024)S(1)} %bitcast.78, f32[8192]{0:T(1024)S(1)} %bitcast.79, f32[8192]{0:T(1024)S(1)} %bitcast.80, f32[8192]{0:T(1024)} %bitcast.81, f32[8192]{0:T(1024)} %bitcast.82, ...), kind=kLoop, calls=%fused_computation.30 | loop fusion | flops 19464192 | bytes 42369024 | tf_op jit(solution)/shard_map/convert_element_type | solution.py:67
  106.1 30.4 %fusion.15 = bf16[192,8192]{0,1:T(8,128)(2,1)S(1)} fusion(f32[198,8192]{0,1:T(8,128)} %get-tuple-element.63, f32[198,8192]{0,1:T(8,128)} %get-tuple-element.64, f32[198,8192]{0,1:T(8,128)} %get-tuple-element.65, bf16[192,8192]{0,1:T(8,128)(2,1)} %copy.15, bf16[198,8192]{0,1:T(8,128)(2,1)S(1)} %get-tuple-element.62, f32[8192]{0:T(1024)S(1)} %bitcast.65, ...), kind=kLoop, calls=%fused_computation.26 | loop fusion | flops 45613056 | bytes 47513600 | tf_op jit(solution)/shard_map/convert_element_type | solution.py:71
  151.1 10.9 %select_bitcast_fusion = bf16[512,64,191]{0,2,1:T(8,128)(2,1)} fusion(bf16[64,191,512]{2,1,0:T(8,128)(2,1)} %reshape.159, pred[64,191]{1,0:T(8,128)(4,1)S(1)} %copy-done.14, pred[64,191]{1,0:T(8,128)(4,1)S(1)} %copy-done.13), kind=kLoop, calls=%fused_computation.8 | loop fusion | flops 12517376 | bytes 25059200 | tf_op jit(solution)/shard_map/jit(_where)/select_n | solution.py:37
  162.0 23.3 %copy.20 = bf16[512,64,191]{2,1,0:T(8,128)(2,1)} copy(bf16[512,64,191]{0,2,1:T(8,128)(2,1)} %select_bitcast_fusion) | data formatting | bytes 25034752 | tf_op jit(solution)/shard_map/while | solution.py:53
  185.5 18.0 %collective-permute-done.1 = bf16[129,8192]{1,0:T(8,128)(2,1)} collective-permute-done((bf16[129,8192]{1,0:T(8,128)(2,1)S(1)}, bf16[129,8192]{1,0:T(8,128)(2,1)}, u32[]{:S(2)}, u32[]{:S(2)}) %collective-permute-start.1) | collective-permute-done | bytes 2113568 | tf_op jit(solution)/shard_map/ppermute | solution.py:10
  203.5 5.6 copy.19
  209.0 6.9 %fusion.3 = f32[321]{0:T(512)S(1)} fusion(bf16[192,8192]{0,1:T(8,128)(2,1)} %copy-done.2, bf16[129,8192]{0,1:T(8,128)(2,1)} %copy.19), kind=kLoop, calls=%fused_computation.6 | loop fusion | flops 15777471 | bytes 5260548 | tf_op jit(solution)/shard_map/reduce_sum | solution.py:15
  216.0 6.7 %fusion.4 = f32[321,8192]{0,1:T(8,128)} fusion(f32[8192]{0:T(1024)S(1)} %bitcast.73, f32[321]{0:T(512)S(1)} %add_rsqrt_fusion, bf16[192,8192]{0,1:T(8,128)(2,1)S(1)} %copy-done.3, bf16[129,8192]{0,1:T(8,128)(2,1)S(1)} %copy-done.5), kind=kLoop, calls=%fused_computation.7 | loop fusion | flops 15777792 | bytes 15811844 | tf_op jit(solution)/shard_map/mul | solution.py:16
  222.7 27.4 %fusion.23 = (f32[319,8192]{0,1:T(8,128)}, bf16[319,8192]{0,1:T(8,128)(2,1)}, f32[319,8192]{0,1:T(8,128)}, f32[319,8192]{0,1:T(8,128)}) fusion(f32[321,8192]{0,1:T(8,128)} %fusion.4, f32[8192]{0:T(1024)S(1)} %bitcast.67, f32[8192]{0:T(1024)S(1)} %bitcast.68, f32[8192]{0:T(1024)S(1)} %bitcast.69, f32[8192]{0:T(1024)S(1)} %bitcast.70, f32[8192]{0:T(1024)S(1)} %bitcast.71, ...), kind=kLoop, calls=%fused_computation.48 | loop fusion | flops 31358976 | bytes 68141056 | tf_op jit(solution)/shard_map/slice | solution.py:63
  250.1 351.6 %while.10 = (s32[]{:T(128)}, f32[3,64,512,16]{1,0,3,2:T(4,128)}, s32[3]{0:T(128)S(1)}, bf16[319,512,16]{0,2,1:T(8,128)(2,1)}, bf16[512,64,191]{2,1,0:T(8,128)(2,...) while((s32[]{:T(128)}, f32[3,64,512,16]{1,0,3,2:T(4,128)}, s32[3]{0:T(128)S(1)}, ...), condition=%wide.region_3.4_spmd, body=%wide.region_2.3_spmd.sunk | while | flops 200278016 | bytes 27263136 | solution.py:53
  251.5 11.3 %fusion.35 = f32[512,16,64]{2,1,0:T(8,128)} fusion(bf16[512,64,191]{2,1,0:T(8,128)(2,1)} %get-tuple-element.152, bf16[319,512,16]{0,2,1:T(8,128)(2,1)} %get-tuple-element.151, s32[]{:T(128)S(6)} %select_n.46), kind=kOutput, calls=%fused_computation.1.clone.1 | convolution fusion | flops 200278016 | bytes 23068676 | tf_op jit(solution)/shard_map/while/body/eval_jaxpr/gij,jgc->igc/dot_general | solution.py:49
  262.8 104.7 %dynamic_update_slice.5 = f32[3,64,512,16]{1,0,3,2:T(4,128)} dynamic-update-slice(f32[3,64,512,16]{1,0,3,2:T(4,128)} %get-tuple-element.140, f32[1,64,512,16]{1,0,3,2:T(1,128)} %bitcast.55, s32[]{:T(128)} %get-tuple-element.139, s32[]{:T(128)} %constant.26.clone.1..sunk, s32[]{:T(128)} %constant.26.clone.1..sunk, s32[]{:T(128)} %constant.26.clone.1..sunk) | dynamic-update-slice | bytes 4194308 | tf_op jit(solution)/shard_map/while/body/jit(dynamic_update_index_in_dim)/dynamic_update_slice | solution.py:53
  368.9 11.3 %fusion.35 = f32[512,16,64]{2,1,0:T(8,128)} fusion(bf16[512,64,191]{2,1,0:T(8,128)(2,1)} %get-tuple-element.152, bf16[319,512,16]{0,2,1:T(8,128)(2,1)} %get-tuple-element.151, s32[]{:T(128)S(6)} %select_n.46), kind=kOutput, calls=%fused_computation.1.clone.1 | convolution fusion | flops 200278016 | bytes 23068676 | tf_op jit(solution)/shard_map/while/body/eval_jaxpr/gij,jgc->igc/dot_general | solution.py:49
  380.2 104.7 %dynamic_update_slice.5 = f32[3,64,512,16]{1,0,3,2:T(4,128)} dynamic-update-slice(f32[3,64,512,16]{1,0,3,2:T(4,128)} %get-tuple-element.140, f32[1,64,512,16]{1,0,3,2:T(1,128)} %bitcast.55, s32[]{:T(128)} %get-tuple-element.139, s32[]{:T(128)} %constant.26.clone.1..sunk, s32[]{:T(128)} %constant.26.clone.1..sunk, s32[]{:T(128)} %constant.26.clone.1..sunk) | dynamic-update-slice | bytes 4194308 | tf_op jit(solution)/shard_map/while/body/jit(dynamic_update_index_in_dim)/dynamic_update_slice | solution.py:53
  486.3 10.7 %fusion.35 = f32[512,16,64]{2,1,0:T(8,128)} fusion(bf16[512,64,191]{2,1,0:T(8,128)(2,1)} %get-tuple-element.152, bf16[319,512,16]{0,2,1:T(8,128)(2,1)} %get-tuple-element.151, s32[]{:T(128)S(6)} %select_n.46), kind=kOutput, calls=%fused_computation.1.clone.1 | convolution fusion | flops 200278016 | bytes 23068676 | tf_op jit(solution)/shard_map/while/body/eval_jaxpr/gij,jgc->igc/dot_general | solution.py:49
  497.0 104.7 %dynamic_update_slice.5 = f32[3,64,512,16]{1,0,3,2:T(4,128)} dynamic-update-slice(f32[3,64,512,16]{1,0,3,2:T(4,128)} %get-tuple-element.140, f32[1,64,512,16]{1,0,3,2:T(1,128)} %bitcast.55, s32[]{:T(128)} %get-tuple-element.139, s32[]{:T(128)} %constant.26.clone.1..sunk, s32[]{:T(128)} %constant.26.clone.1..sunk, s32[]{:T(128)} %constant.26.clone.1..sunk) | dynamic-update-slice | bytes 4194308 | tf_op jit(solution)/shard_map/while/body/jit(dynamic_update_index_in_dim)/dynamic_update_slice | solution.py:53
  601.7 18.9 %reshape.153 = f32[192,8192]{0,1:T(8,128)} reshape(f32[3,64,512,16]{1,0,3,2:T(4,128)} %get-tuple-element.32) | data formatting | bytes 12582912 | tf_op jit(solution)/shard_map/reshape | solution.py:54
  620.6 20.0 %fusion.10 = bf16[192,8192]{0,1:T(8,128)(2,1)} fusion(f32[192,8192]{0,1:T(8,128)} %reshape.153, f32[319,8192]{0,1:T(8,128)} %get-tuple-element.60, f32[319,8192]{0,1:T(8,128)} %get-tuple-element.61, f32[319,8192]{0,1:T(8,128)} %get-tuple-element.58, bf16[192,8192]{0,1:T(8,128)(2,1)} %copy-done.2, f32[8192]{0:T(1024)S(1)} %bitcast.76, f32[8192]{0:T(1024)S(1)} %bitcast.77, ...), kind=kLoop, calls=%fused_computation.18 | loop fusion | flops 14155776 | bytes 31555584 | tf_op jit(solution)/shard_map/convert_element_type | solution.py:71
  640.5 6.0 copy.22
  (57 shorter events, 27.9 us)
Async XLA Ops:
  0.0 15.3 %copy-start = (bf16[1,128,512]{2,1,0:T(8,128)(2,1)S(1)}, bf16[1,128,512]{2,1,0:T(8,128)(2,1)}, u32[]{:S(2)}) copy-start(bf16[1,128,512]{2,1,0:T(8,128)(2,1)} %param.11) | copy-start | bytes 393220
  0.0 14.3 %copy-start.15 = (f32[1,2,8192]{2,1,0:T(2,128)S(1)}, f32[1,2,8192]{2,1,0:T(2,128)}, u32[]{:S(2)}) copy-start(f32[1,2,8192]{2,1,0:T(2,128)} %param.8) | copy-start | bytes 196612
  0.0 15.0 %copy-start.8 = (f32[1,7,8192]{2,0,1:T(1,128)S(1)}, f32[1,7,8192]{2,0,1:T(1,128)}, u32[]{:S(2)}) copy-start(f32[1,7,8192]{2,0,1:T(1,128)} %param.10) | copy-start | bytes 688132
  1.0 77.7 %collective-permute-start = (bf16[8,8192]{1,0:T(8,128)(2,1)S(1)}, bf16[8,8192]{1,0:T(8,128)(2,1)S(1)}, u32[]{:S(2)}, u32[]{:S(2)}) collective-permute-start(bf16[8,8192]{1,0:T(8,128)(2,1)S(1)} %slice.163), channel_id=1, source_target_pairs={{0,1},{1,2},{2,3},{3,4},{4,5},{5,6},{6,7},{7,8},{8,9},{9,10},{10,1... | collective-permute-start | bytes 393224 | tf_op jit(solution)/shard_map/ppermute | solution.py:10
  78.0 6.7 %copy-start.9 = (f32[1,1,8192]{2,1,0:T(1,128)S(1)}, f32[1,1,8192]{2,1,0:T(1,128)}, u32[]{:S(2)}) copy-start(f32[1,1,8192]{2,1,0:T(1,128)} %get-tuple-element.93) | copy-start | bytes 98308
  79.7 4.9 copy-start.6
  79.7 5.0 copy-start.4
  84.6 5.8 copy-start.10
  84.6 5.8 copy-start.11
  84.7 5.8 copy-start.12
  136.5 2.0 copy-start.2
  138.5 12.5 %copy-start.13 = (pred[64,191]{1,0:T(8,128)(4,1)S(1)}, pred[64,191]{1,0:T(8,128)(4,1)}, u32[]{:S(2)}) copy-start(pred[64,191]{1,0:T(8,128)(4,1)} %get-tuple-element.95) | copy-start | bytes 36676
  138.5 12.6 %copy-start.14 = (pred[64,191]{1,0:T(8,128)(4,1)S(1)}, pred[64,191]{1,0:T(8,128)(4,1)}, u32[]{:S(2)}) copy-start(pred[64,191]{1,0:T(8,128)(4,1)} %get-tuple-element.96) | copy-start | bytes 36676
  147.3 56.1 %collective-permute-start.1 = (bf16[129,8192]{1,0:T(8,128)(2,1)S(1)}, bf16[129,8192]{1,0:T(8,128)(2,1)}, u32[]{:S(2)}, u32[]{:S(2)}) collective-permute-start(bf16[129,8192]{1,0:T(8,128)(2,1)S(1)} %copy.18), channel_id=1, source_target_pairs={{0,1},{1,2},{2,3},{3,4},{4,5},{5,6},{6,7},{7,8},{8,9},{9,10},{10,1... | collective-permute-start | bytes 6340616 | tf_op jit(solution)/shard_map/ppermute | solution.py:10
  162.0 23.3 %copy-start.7 = (f32[3,3,8192]{2,1,0:T(4,128)S(1)}, f32[3,3,8192]{2,1,0:T(4,128)}, u32[]{:S(2)}) copy-start(f32[3,3,8192]{2,1,0:T(4,128)} %get-tuple-element.97) | copy-start | bytes 884740
  209.0 6.9 %copy-start.3 = (bf16[192,8192]{0,1:T(8,128)(2,1)S(1)}, bf16[192,8192]{0,1:T(8,128)(2,1)}, u32[]{:S(2)}) copy-start(bf16[192,8192]{0,1:T(8,128)(2,1)} %copy-done.2) | copy-start | bytes 9437188
  209.0 7.0 %copy-start.5 = (bf16[129,8192]{0,1:T(8,128)(2,1)S(1)}, bf16[129,8192]{0,1:T(8,128)(2,1)}, u32[]{:S(2)}) copy-start(bf16[129,8192]{0,1:T(8,128)(2,1)} %copy.19) | copy-start | bytes 6340612
  620.6 26.0 %copy-start.1 = (bf16[1,128,512]{2,1,0:T(8,128)(2,1)S(1)}, bf16[1,128,512]{2,1,0:T(8,128)(2,1)}, u32[]{:S(2)}) copy-start(bf16[1,128,512]{2,1,0:T(8,128)(2,1)} %param.11) | copy-start | bytes 393220
where the time goes:
time: 657 us; the launch traced here: 647 us
  local copies, waits for them, and re-layouts  456 us (69%)
  other arithmetic  129 us (20%)
  matrix products  33.4 us (5%)
  waiting for transfers between devices  18 us (3%)
  starting transfers between devices  7.27 us (1%)
    dynamic_update_slice x3, local copies, waits for them, and re-layouts, long_filter(): stacked = lax.map(block_out, jnp.arange(out_rows // 64))  314 us
    gather x2, local copies, waits for them, and re-layouts, build_table(): jnp.take(filter_taps.T, jnp.clip(lag_index, 0, tap_count - 1), axis=1)  62.7 us
    convert_element_type x2, other arithmetic, apply_operator(): return (residual + gate_rows * filtered).astype(jnp.bfloat16)  50.4 us
    dot_general x3, matrix products, block_out(): jnp.einsum('gij,jgc->igc', long_table, window_rows, preferred_element_typ...  33.4 us
    slice x1, other arithmetic, apply_operator(): summed = feature_taps[j, 0] * scaled[lead_rows:]  27.4 us
    while x1, local copies, waits for them, and re-layouts, long_filter(): stacked = lax.map(block_out, jnp.arange(out_rows // 64))  23.3 us
    reshape x1, local copies, waits for them, and re-layouts, long_filter(): return stacked.reshape(out_rows, product.shape[1])  18.9 us
    ppermute x2, waiting for transfers between devices, from_behind(): return lax.ppermute(x, axis, pairs)  18 us
  transfers between devices with their start and end apart: 2, of which 1 were waited for; matrix products, arithmetic and copies ran while one was open for 17% of the time, Pallas kernels for 0%

commit v1 on v0

v1 whole, which is shorter than its diff:
```python
import functools

import jax
import jax.numpy as jnp
import numpy as np
from jax import lax
from jax.experimental import pallas as pl
from jax.experimental.pallas import tpu as pltpu
from jax.sharding import PartitionSpec as P

F32 = jnp.float32
BF16 = jnp.bfloat16
EDGE = 16
HALO = 144
REACH = 128
POINTS = 256
PAD = 8
LANES = 128
WIDE = 256
STEP = 16
EPS = 1e-06
CHUNKS = ((0, 6144), (6144, 2048))
VMEM_LIMIT = 48 * 1024 * 1024


def transform_tables():
    k = np.arange(POINTS // 2)[:, None]
    n = np.arange(POINTS)[None, :]
    angle = np.pi * ((2 * k + 1) * n % (2 * POINTS)) / POINTS
    forward = np.concatenate([np.cos(angle), -np.sin(angle)], axis=0)
    backward = forward.T * (2.0 / POINTS)
    return jnp.asarray(forward, BF16), jnp.asarray(backward, BF16)


def params(vmem=VMEM_LIMIT):
    return pltpu.CompilerParams(vmem_limit_bytes=vmem)


def tap_rows(gain, feat_ref, lanes):
    return [
        [feat_ref[0, 0, j, i : i + 1, lanes] * gain for i in range(3)] for j in range(3)
    ]


def three_taps(scaled_ref, at, taps):
    summed = taps[0] * scaled_ref[pl.ds(at, STEP), :]
    for i in range(1, 3):
        summed = summed + taps[i] * scaled_ref[pl.ds(at - i, STEP), :]
    return summed


def se_filter(product_ref, at, taps):
    summed = taps[0] * product_ref[pl.ds(at, STEP), :]
    for i in range(1, len(taps)):
        summed = summed + taps[i] * product_ref[pl.ds(at - i, STEP), :]
    return summed


def to_row(column, width):
    rows = column.shape[0]
    on = lax.broadcasted_iota(jnp.int32, (rows, width), 0) == lax.broadcasted_iota(
        jnp.int32, (rows, width), 1
    )
    return jnp.sum(jnp.where(on, column, 0.0), axis=0, keepdims=True)


def to_column(row, start, rows):
    width = row.shape[1]
    on = lax.broadcasted_iota(jnp.int32, (rows, width), 0) + start == lax.broadcasted_iota(
        jnp.int32, (rows, width), 1
    )
    return jnp.sum(jnp.where(on, row, 0.0), axis=1, keepdims=True)


def taps_transform_kernel(taps_ref, forward_ref, out_ref):
    wide = out_ref.shape[1]
    groups = taps_ref.shape[1]
    channels = lax.broadcasted_iota(jnp.int32, (groups, wide), 1)
    channels = channels + pl.program_id(0) * wide
    group = lax.broadcasted_iota(jnp.int32, (groups, wide), 0)
    spread = jnp.where((channels >= group * 16) & (channels < group * 16 + 16), 1.0, 0.0)
    full = jnp.dot(taps_ref[...], spread.astype(BF16), preferred_element_type=F32)
    out_ref[...] = jnp.dot(
        forward_ref[...], full.astype(BF16), preferred_element_type=F32
    ).astype(BF16)


def own_se_kernel(
    tokens_ref, edge_ref, gain_ref, feat_ref, se_ref,
    mid_ref, inv_ref, stat_ref,
    first_inv, square, scaled, product,
):
    rows, width = tokens_ref.shape
    total = rows + EDGE
    tiles = width // LANES

    def lanes_of(j):
        return pl.ds(pl.multiple_of(j * LANES, LANES), LANES)

    def read(at, lanes):
        if at < EDGE:
            return edge_ref[at : at + STEP, lanes].astype(F32)
        return tokens_ref[at - EDGE : at - EDGE + STEP, lanes].astype(F32)

    square[...] = jnp.zeros_like(square)

    def add_squares(j, carry):
        lanes = lanes_of(j)
        for at in range(0, total, STEP):
            x = read(at, lanes)
            square[at : at + STEP, :] += x * x
        return carry

    lax.fori_loop(0, tiles, add_squares, 0)
    first = lax.rsqrt(jnp.sum(square[...], axis=1, keepdims=True) / width + EPS)
    first_inv[...] = jnp.broadcast_to(first, first_inv.shape)
    square[...] = jnp.zeros_like(square)
    scaled[0:PAD, :] = jnp.zeros((PAD, LANES), F32)
    product[0:PAD, :] = jnp.zeros((PAD, LANES), F32)

    def one_tile(j, carry):
        lanes = lanes_of(j)
        taps = tap_rows(gain_ref[0, 0:1, lanes], feat_ref, lanes)
        filter_taps = [se_ref[0, i : i + 1, lanes] for i in range(7)]
        for at in range(0, total, STEP):
            x = read(at, lanes)
            scaled[PAD + at : PAD + at + STEP, :] = x * first_inv[at : at + STEP, :]
        for at in range(0, total, STEP):
            k = three_taps(scaled, PAD + at, taps[1])
            v = three_taps(scaled, PAD + at, taps[2])
            product[PAD + at : PAD + at + STEP, :] = (k * v).astype(BF16).astype(F32)
        for at in range(0, total, STEP):
            q = three_taps(scaled, PAD + at, taps[0])
            f = se_filter(product, PAD + at, filter_taps)
            result = (read(at, lanes) + q * f).astype(BF16)
            mid_ref[at : at + STEP, lanes] = result
            wide_result = result.astype(F32)
            square[at : at + STEP, :] += wide_result * wide_result
        return carry

    lax.fori_loop(0, tiles, one_tile, 0)
    second = lax.rsqrt(jnp.sum(square[...], axis=1, keepdims=True) / width + EPS)
    inv_ref[...] = jnp.broadcast_to(second, inv_ref.shape)
    stat_ref[...] = jnp.zeros_like(stat_ref)
    stat_ref[0:1, :] = to_row(first[EDGE:], stat_ref.shape[1])
    stat_ref[1:2, :] = to_row(second[EDGE:], stat_ref.shape[1])


def multiply_spectra(spectrum, taps_ref, out_ref):
    half = POINTS // 2
    for at in range(0, half, STEP):
        a, b = spectrum[at : at + STEP], spectrum[half + at : half + at + STEP]
        c = taps_ref[at : at + STEP, :].astype(F32)
        d = taps_ref[half + at : half + at + STEP, :].astype(F32)
        out_ref[at : at + STEP, :] = (a * c - b * d).astype(BF16)
        out_ref[half + at : half + at + STEP, :] = (a * d + b * c).astype(BF16)


def own_mr_kernel(
    mid_ref, inv_ref, gain_ref, feat_ref, table_ref, forward_ref, backward_ref,
    out_ref, base_ref, gate_ref,
    scaled, product, gate, spectrum, late_spectrum,
):
    total = mid_ref.shape[0]
    rows = total - EDGE
    for half in range(WIDE // LANES):
        lanes = pl.ds(half * LANES, LANES)
        taps = tap_rows(gain_ref[0, 1:2, lanes], feat_ref, lanes)
        for at in range(0, total, STEP):
            scaled[at : at + STEP, :] = (
                mid_ref[at : at + STEP, lanes].astype(F32) * inv_ref[at : at + STEP, :]
            )
        for at in range(0, rows, STEP):
            k = three_taps(scaled, EDGE + at, taps[1])
            v = three_taps(scaled, EDGE + at, taps[2])
            product[at : at + STEP, lanes] = (k * v).astype(BF16)
            gate[at : at + STEP, lanes] = three_taps(scaled, EDGE + at, taps[0])
    early = jnp.dot(
        forward_ref[:, REACH:], product[0:REACH, :], preferred_element_type=F32
    )
    late = jnp.dot(
        forward_ref[:, 0:rows], product[...], preferred_element_type=F32
    )
    multiply_spectra(early, table_ref, spectrum)
    multiply_spectra(late, table_ref, late_spectrum)
    first = jnp.dot(backward_ref[REACH:, :], spectrum[...], preferred_element_type=F32)
    last = jnp.dot(
        backward_ref[REACH:rows, :], late_spectrum[...], preferred_element_type=F32
    )
    for at in range(0, REACH, STEP):
        q = gate[at : at + STEP, :]
        h = mid_ref[EDGE + at : EDGE + at + STEP, :].astype(F32)
        base_ref[at : at + STEP, :] = h + q * first[at : at + STEP]
        gate_ref[at : at + STEP, :] = q
    for at in range(0, rows - REACH, STEP):
        q = gate[REACH + at : REACH + at + STEP, :]
        h = mid_ref[EDGE + REACH + at : EDGE + REACH + at + STEP, :].astype(F32)
        out_ref[at : at + STEP, :] = (h + q * last[at : at + STEP]).astype(BF16)


def halo_kernel(
    main_ref, edge_ref, stat_ref, gain_ref, feat_first_ref, se_ref, feat_ref, table_ref,
    forward_ref, backward_ref, base_ref, gate_ref, held_ref,
    out_ref,
    first_inv, second_inv, scaled, se_product, again, product, spectrum,
):
    del held_ref
    main_rows = main_ref.shape[0]
    own_rows = base_ref.shape[0] + 64

    @pl.when(pl.program_id(0) == 0)
    def _():
        start = own_rows - HALO
        first_inv[...] = jnp.broadcast_to(
            to_column(stat_ref[0:1, :], start, HALO), first_inv.shape
        )
        second_inv[...] = jnp.broadcast_to(
            to_column(stat_ref[1:2, :], start, HALO), second_inv.shape
        )
        scaled[0:PAD, :] = jnp.zeros((PAD, LANES), F32)
        se_product[0:PAD, :] = jnp.zeros((PAD, LANES), F32)

    def read(at, lanes):
        if at < main_rows:
            return main_ref[at : at + STEP, lanes].astype(F32)
        return edge_ref[at - main_rows : at - main_rows + STEP, lanes].astype(F32)

    for half in range(WIDE // LANES):
        lanes = pl.ds(half * LANES, LANES)
        taps = tap_rows(gain_ref[0, 0:1, lanes], feat_first_ref, lanes)
        filter_taps = [se_ref[0, i : i + 1, lanes] for i in range(7)]
        late_taps = tap_rows(gain_ref[0, 1:2, lanes], feat_ref, lanes)
        for at in range(0, HALO, STEP):
            scaled[PAD + at : PAD + at + STEP, :] = (
                read(at, lanes) * first_inv[at : at + STEP, :]
            )
        for at in range(0, HALO, STEP):
            k = three_taps(scaled, PAD + at, taps[1])
            v = three_taps(scaled, PAD + at, taps[2])
            se_product[PAD + at : PAD + at + STEP, :] = (k * v).astype(BF16).astype(F32)
        for at in range(0, HALO, STEP):
            q = three_taps(scaled, PAD + at, taps[0])
            f = se_filter(se_product, PAD + at, filter_taps)
            result = (read(at, lanes) + q * f).astype(BF16).astype(F32)
            again[at : at + STEP, :] = result * second_inv[at : at + STEP, :]
        for at in range(HALO - REACH, HALO, STEP):
            k = three_taps(again, at, late_taps[1])
            v = three_taps(again, at, late_taps[2])
            to = at - (HALO - REACH)
            product[to : to + STEP, lanes] = (k * v).astype(BF16)
    seen = jnp.dot(
        forward_ref[:, 0:REACH], product[...], preferred_element_type=F32
    )
    multiply_spectra(seen, table_ref, spectrum)
    carried = jnp.dot(
        backward_ref[REACH:, :], spectrum[...], preferred_element_type=F32
    )
    for at in range(0, REACH, STEP):
        out_ref[at : at + STEP, :] = (
            base_ref[at : at + STEP, :]
            + gate_ref[at : at + STEP, :] * carried[at : at + STEP]
        ).astype(BF16)


def whole(array):
    return pl.BlockSpec(array.shape, lambda *_: (0,) * array.ndim)


def on_device(tokens, norm_gain, feat_taps, se_taps, mr_taps):
    rows, width = tokens.shape
    total = rows + EDGE
    tiles = width // WIDE
    forward, backward = transform_tables()
    length = lax.axis_size(("section", "ctx"))

    def from_behind(x):
        pairs = [(i, i + 1) for i in range(length - 1)]
        return lax.ppermute(x, ("section", "ctx"), pairs)

    edge = from_behind(tokens[rows - EDGE :])
    mains = [
        from_behind(tokens[rows - HALO : rows - EDGE, start : start + size])
        for start, size in CHUNKS
    ]

    table = pl.pallas_call(
        taps_transform_kernel,
        grid=(width // 1024,),
        in_specs=[
            whole(mr_taps[0]),
            pl.BlockSpec((POINTS, REACH), lambda j: (0, 0)),
        ],
        out_specs=pl.BlockSpec((POINTS, 1024), lambda j: (0, j)),
        out_shape=jax.ShapeDtypeStruct((POINTS, width), BF16),
        compiler_params=params(),
        name="taps_transform",
    )(mr_taps[0], forward)

    mid, inv, stat = pl.pallas_call(
        own_se_kernel,
        grid=(1,),
        in_specs=[
            whole(tokens),
            whole(edge),
            whole(norm_gain),
            pl.BlockSpec((1, 1, 3, 3, width), lambda i: (0, 0, 0, 0, 0)),
            whole(se_taps),
        ],
        out_specs=[
            pl.BlockSpec((total, width), lambda i: (0, 0)),
            pl.BlockSpec((total, LANES), lambda i: (0, 0)),
            pl.BlockSpec((8, WIDE), lambda i: (0, 0)),
        ],
        out_shape=[
            jax.ShapeDtypeStruct((total, width), BF16),
            jax.ShapeDtypeStruct((total, LANES), F32),
            jax.ShapeDtypeStruct((8, WIDE), F32),
        ],
        scratch_shapes=[
            pltpu.VMEM((total, LANES), F32),
            pltpu.VMEM((total, LANES), F32),
            pltpu.VMEM((PAD + total, LANES), F32),
            pltpu.VMEM((PAD + total, LANES), F32),
        ],
        compiler_params=params(),
        name="own_se",
    )(tokens, edge, norm_gain, feat_taps, se_taps)
    halo_stat = from_behind(stat)

    def feat_spec(which, first):
        return pl.BlockSpec((1, 1, 3, 3, WIDE), lambda j: (0, which, 0, 0, first + j))

    out, base, gate = pl.pallas_call(
        own_mr_kernel,
        grid=(tiles,),
        in_specs=[
            pl.BlockSpec((total, WIDE), lambda j: (0, j)),
            whole(inv),
            pl.BlockSpec((1, 2, WIDE), lambda j: (0, 0, j)),
            feat_spec(1, 0),
            pl.BlockSpec((POINTS, WIDE), lambda j: (0, j)),
            whole(forward),
            whole(backward),
        ],
        out_specs=[
            pl.BlockSpec((rows - REACH, WIDE), lambda j: (REACH // (rows - REACH), j)),
            pl.BlockSpec((REACH, WIDE), lambda j: (0, j)),
            pl.BlockSpec((REACH, WIDE), lambda j: (0, j)),
        ],
        out_shape=[
            jax.ShapeDtypeStruct((rows, width), BF16),
            jax.ShapeDtypeStruct((REACH, width), F32),
            jax.ShapeDtypeStruct((REACH, width), F32),
        ],
        scratch_shapes=[
            pltpu.VMEM((total, LANES), F32),
            pltpu.VMEM((rows, WIDE), BF16),
            pltpu.VMEM((rows, WIDE), F32),
            pltpu.VMEM((POINTS, WIDE), BF16),
            pltpu.VMEM((POINTS, WIDE), BF16),
        ],
        compiler_params=params(),
        name="own_mr",
    )(mid, inv, norm_gain, feat_taps, table, forward, backward)

    for (start, size), main in zip(CHUNKS, mains):
        first = start // WIDE
        out = pl.pallas_call(
            halo_kernel,
            grid=(size // WIDE,),
            in_specs=[
                pl.BlockSpec((HALO - EDGE, WIDE), lambda j: (0, j)),
                pl.BlockSpec((EDGE, WIDE), lambda j, f=first: (0, f + j)),
                whole(halo_stat),
                pl.BlockSpec((1, 2, WIDE), lambda j, f=first: (0, 0, f + j)),
                feat_spec(0, first),
                pl.BlockSpec((1, 7, WIDE), lambda j, f=first: (0, 0, f + j)),
                feat_spec(1, first),
                pl.BlockSpec((POINTS, WIDE), lambda j, f=first: (0, f + j)),
                whole(forward),
                whole(backward),
                pl.BlockSpec((REACH, WIDE), lambda j, f=first: (0, f + j)),
                pl.BlockSpec((REACH, WIDE), lambda j, f=first: (0, f + j)),
                pl.BlockSpec(memory_space=pl.ANY),
            ],
            out_specs=pl.BlockSpec((REACH, WIDE), lambda j, f=first: (0, f + j)),
            out_shape=jax.ShapeDtypeStruct((rows, width), BF16),
            input_output_aliases={12: 0},
            scratch_shapes=[
                pltpu.VMEM((HALO, LANES), F32),
                pltpu.VMEM((HALO, LANES), F32),
                pltpu.VMEM((PAD + HALO, LANES), F32),
                pltpu.VMEM((PAD + HALO, LANES), F32),
                pltpu.VMEM((HALO, LANES), F32),
                pltpu.VMEM((REACH, WIDE), BF16),
                pltpu.VMEM((POINTS, WIDE), BF16),
            ],
            compiler_params=params(),
            name="halo",
        )(
            main, edge, halo_stat, norm_gain, feat_taps, se_taps, feat_taps, table,
            forward, backward, base, gate, out,
        )
    return out


def solution(mesh):
    placed = (P(("section", "ctx"), None), P(), P(), P(), P())
    return jax.shard_map(
        on_device,
        mesh=mesh,
        in_specs=placed,
        out_specs=P(("section", "ctx"), None),
        check_vma=False,
    )
```

time: 657 us -> 145 us (0.22); the launches traced: 647 us -> 144 us
  local copies, waits for them, and re-layouts: 456 us -> 5.06 us
  other arithmetic: 129 us -> 0 us
  Pallas kernels: 0 us -> 77.8 us
  matrix products: 33.4 us -> 0 us
  waiting for transfers between devices: 18 us -> 47.9 us
    dynamic_update_slice x3 -> x0, local copies, waits for them, and re-layouts: 314 us -> none  [long_filter(): stacked = lax.map(block_out, jnp.arange(out_rows // 64))]
    pallas_call x0 -> x5, Pallas kernels: none -> 77.8 us  [the longest x2 31.7 us: on_device(): pl.pallas_call(halo_kernel, grid=(size // WIDE,), in_specs=[pl.BlockSpec(...]
    convert_element_type x3 -> x0, other arithmetic: 66 us -> none  [the longest x2 50.4 us: apply_operator(): return (residual + gate_rows * filtered).astype(jnp.bfloat16)]
    gather x2 -> x0, local copies, waits for them, and re-layouts: 62.7 us -> none  [build_table(): jnp.take(filter_taps.T, jnp.clip(lag_index, 0, tap_count - 1), axis=1)]
    dot_general x3 -> x0, matrix products: 33.4 us -> none  [block_out(): jnp.einsum('gij,jgc->igc', long_table, window_rows, preferred_element_typ...]
    ppermute x2 -> x4, waiting for transfers between devices: 18 us -> 47.9 us  [from_behind(): return lax.ppermute(x, ('section', 'ctx'), pairs)]
    slice x1 -> x0, other arithmetic: 27.4 us -> none  [apply_operator(): summed = feature_taps[j, 0] * scaled[lead_rows:]]
    while x1 -> x0, local copies, waits for them, and re-layouts: 23.3 us -> none  [long_filter(): stacked = lax.map(block_out, jnp.arange(out_rows // 64))]
  transfers between devices with their start and end apart: 2 -> 4, of which waited for: 1 -> 1; matrix products, arithmetic and copies ran while one was open for 17% -> 1% of each run, Pallas kernels for 0% -> 48%
where the time goes in v1:
time: 145 us; the launch traced here: 144 us
  Pallas kernels  77.8 us (54%)
  waiting for transfers between devices  47.9 us (33%)
  starting transfers between devices  12.6 us (9%)
  local copies, waits for them, and re-layouts  5.06 us (3%)
    ppermute x4, waiting for transfers between devices, from_behind(): return lax.ppermute(x, ('section', 'ctx'), pairs)  47.9 us
    pallas_call x2, Pallas kernels, on_device(): pl.pallas_call(halo_kernel, grid=(size // WIDE,), in_specs=[pl.BlockSpec(...  31.7 us
    pallas_call x1, Pallas kernels, on_device(): pl.pallas_call(own_mr_kernel, grid=(tiles,), in_specs=[pl.BlockSpec((tota...  25.8 us
    pallas_call x1, Pallas kernels, on_device(): pl.pallas_call(own_se_kernel, grid=(1,), in_specs=[whole(tokens), whole(e...  14.2 us
    ppermute x4, starting transfers between devices, from_behind(): return lax.ppermute(x, ('section', 'ctx'), pairs)  12.6 us
    pallas_call x1, Pallas kernels, on_device(): pl.pallas_call(taps_transform_kernel, grid=(width // 1024,), in_specs=[wh...  6.15 us
  transfers between devices with their start and end apart: 4, of which 1 were waited for; matrix products, arithmetic and copies ran while one was open for 1% of the time, Pallas kernels for 48%

profile of v1, /device:TPU:7, one launch (start us, length us, event | category | flops | bytes accessed | tf_op | source)
XLA Modules:
  0.0 143.6 jit_solution(5414657571867597020)
XLA Ops:
  0.0 1.7 %slice.11 = bf16[128,6144]{1,0:T(8,128)(2,1)S(1)} slice(bf16[192,8192]{1,0:T(8,128)(2,1)} %tokens_ref.1), slice={[48:176], [0:6144]} | slice | bytes 3145728 | tf_op jit(solution)/shard_map/slice | solution.py:282
  1.7 3.5 %collective-permute-start.3 = (bf16[128,6144]{1,0:T(8,128)(2,1)S(1)}, bf16[128,6144]{1,0:T(8,128)(2,1)S(1)}, u32[]{:S(2)}, u32[]{:S(2)}) collective-permute-start(bf16[128,6144]{1,0:T(8,128)(2,1)S(1)} %slice.11), channel_id=1, source_target_pairs={{0,1},{1,2},{2,3},{3,4},{4,5},{5,6},{6,7},{7,8},{8,9},{9,10},{10,1... | collective-permute-start | bytes 4718600 | tf_op jit(solution)/shard_map/ppermute | solution.py:278
  5.2 0.0 copy-done.1
  5.2 0.9 slice.9
  6.1 3.5 %collective-permute-start = (bf16[128,2048]{1,0:T(8,128)(2,1)}, bf16[128,2048]{1,0:T(8,128)(2,1)S(1)}, u32[]{:S(2)}, u32[]{:S(2)}) collective-permute-start(bf16[128,2048]{1,0:T(8,128)(2,1)} %slice.9), channel_id=1, source_target_pairs={{0,1},{1,2},{2,3},{3,4},{4,5},{5,6},{6,7},{7,8},{8,9},{9,10},{10,1... | collective-permute-start | bytes 1572872 | tf_op jit(solution)/shard_map/ppermute | solution.py:278
  9.7 0.0 copy-start.3
  9.7 0.0 copy-start.6
  9.7 3.4 %collective-permute-start.1 = (bf16[16,8192]{1,0:T(8,128)(2,1)S(1)}, bf16[16,8192]{1,0:T(8,128)(2,1)S(1)}, u32[]{:S(2)}, u32[]{:S(2)}) collective-permute-start(bf16[16,8192]{1,0:T(8,128)(2,1)S(1)} %slice.10), channel_id=1, source_target_pairs={{0,1},{1,2},{2,3},{3,4},{4,5},{5,6},{6,7},{7,8},{8,9},{9,10},{10,1... | collective-permute-start | bytes 786440 | tf_op jit(solution)/shard_map/ppermute | solution.py:278
  13.1 0.0 copy-done.7
  13.1 0.4 copy.10.feat_ref.feat_first_ref
  13.5 0.0 copy-done.8
  13.5 0.1 copy.11.se_ref
  13.7 47.9 %collective-permute-done.1.edge_ref = bf16[16,8192]{1,0:T(8,128)(2,1)S(1)} collective-permute-done((bf16[16,8192]{1,0:T(8,128)(2,1)S(1)}, bf16[16,8192]{1,0:T(8,128)(2,1)S(1)}, u32[]{:S(2)}, u32[]{:S(2)}) %collective-permute-start.1) | collective-permute-done | bytes 262176 | tf_op jit(solution)/shard_map/ppermute | solution.py:278
  61.6 0.0 copy-done.5
  61.6 14.2 %own_se.1 = (bf16[208,8192]{1,0:T(8,128)(2,1)}, f32[208,128]{1,0:T(8,128)S(1)}, f32[8,256]{1,0:T(8,128)S(1)}) custom-call(bf16[192,8192]{1,0:T(8,128)(2,1)S(1)} %copy-done.1, bf16[16,8192]{1,0:T(8,128)(2,1)S(1)} %collective-permute-done.1.edge_ref, f32[1,2,8192]{2,1,0:T(2,128)S(1)} %copy-done.5, f32[1,2,3,3,8192]{4,3,2,1,0:T(4,128)S(1)} %copy.10.feat_ref.feat_first_ref, ...), custom_call_target="tpu_custom_call" | custom-call | tf_op jit(solution)/shard_map/own_se/pallas_call | solution.py:299
  75.7 2.2 %collective-permute-start.2 = (f32[8,256]{1,0:T(8,128)S(1)}, f32[8,256]{1,0:T(8,128)S(1)}, u32[]{:S(2)}, u32[]{:S(2)}) collective-permute-start(f32[8,256]{1,0:T(8,128)S(1)} %get-tuple-element.11), channel_id=1, source_target_pairs={{0,1},{1,2},{2,3},{3,4},{4,5},{5,6},{6,7},{7,8},{8,9},{9,10},{10,1... | collective-permute-start | bytes 24584 | tf_op jit(solution)/shard_map/ppermute | solution.py:278
  77.9 6.2 %taps_transform.1.table_ref = bf16[256,8192]{1,0:T(8,128)(2,1)S(1)} custom-call(bf16[128,512]{1,0:T(8,128)(2,1)S(1)} %bitcast.1, bf16[256,256]{1,0:T(8,128)(2,1)S(1)} %copy-done.3), custom_call_target="tpu_custom_call" | custom-call | tf_op jit(solution)/shard_map/taps_transform/pallas_call | solution.py:286
  84.1 1.9 %copy-done = bf16[256,8192]{1,0:T(8,128)(2,1)} copy-done((bf16[256,8192]{1,0:T(8,128)(2,1)}, bf16[256,8192]{1,0:T(8,128)(2,1)S(1)}, u32[]{:S(2)}) %copy-start) | copy-done | bytes 4194328
  86.1 25.8 %own_mr.1 = (bf16[192,8192]{1,0:T(8,128)(2,1)}, f32[128,8192]{1,0:T(8,128)}, f32[128,8192]{1,0:T(8,128)}) custom-call(bf16[208,8192]{1,0:T(8,128)(2,1)S(1)} %copy-done.2, f32[208,128]{1,0:T(8,128)S(1)} %get-tuple-element.13.inv_ref, f32[1,2,8192]{2,1,0:T(2,128)S(1)} %copy-done.5, f32[1,2,3,3,8192]{4,3,2,1,0:T(4,128)S(1)} %copy.10.feat_ref.feat_first_ref, ...), custom_call_target="tpu_custom_call" | custom-call | tf_op jit(solution)/shard_map/own_mr/pallas_call | solution.py:333
  111.8 0.0 collective-permute-done.2.stat_ref
  111.8 0.0 collective-permute-done.3.main_ref
  111.8 23.0 %halo.2.held_ref = bf16[192,8192]{1,0:T(8,128)(2,1)} custom-call(bf16[128,6144]{1,0:T(8,128)(2,1)S(1)} %collective-permute-done.3.main_ref, bf16[16,8192]{1,0:T(8,128)(2,1)S(1)} %collective-permute-done.1.edge_ref, f32[8,256]{1,0:T(8,128)S(1)} %collective-permute-done.2.stat_ref, f32[1,2,8192]{2,1,0:T(2,128)S(1)} %copy-done.5, ...), custom_call_target="tpu_custom_call", output_to_operand_aliasing={{}: (12, {})} | custom-call | tf_op jit(solution)/shard_map/halo/pallas_call | solution.py:368
  134.9 0.0 collective-permute-done.main_ref
  134.9 8.7 %halo.3 = bf16[192,8192]{1,0:T(8,128)(2,1)} custom-call(bf16[128,2048]{1,0:T(8,128)(2,1)S(1)} %collective-permute-done.main_ref, bf16[16,8192]{1,0:T(8,128)(2,1)S(1)} %collective-permute-done.1.edge_ref, f32[8,256]{1,0:T(8,128)S(1)} %collective-permute-done.2.stat_ref, f32[1,2,8192]{2,1,0:T(2,128)S(1)} %copy-done.5, ...), custom_call_target="tpu_custom_call", output_to_operand_aliasing={{}: (12, {})} | custom-call | tf_op jit(solution)/shard_map/halo/pallas_call | solution.py:368
  (12 shorter events, 0.0 us)
Async XLA Ops:
  0.0 5.2 %copy-start.1 = (bf16[192,8192]{1,0:T(8,128)(2,1)S(1)}, bf16[192,8192]{1,0:T(8,128)(2,1)}, u32[]{:S(2)}) copy-start(bf16[192,8192]{1,0:T(8,128)(2,1)} %tokens_ref.1) | copy-start | bytes 9437188
  0.0 13.1 %copy-start.7 = (f32[1,2,3,3,8192]{4,1,3,2,0:T(2,128)S(1)}, f32[1,2,3,3,8192]{4,1,3,2,0:T(2,128)}, u32[]{:S(2)}) copy-start(f32[1,2,3,3,8192]{4,1,3,2,0:T(2,128)} %param.9) | copy-start | bytes 1769476
  0.0 13.5 %copy-start.8 = (f32[1,7,8192]{2,0,1:T(1,128)S(1)}, f32[1,7,8192]{2,0,1:T(1,128)}, u32[]{:S(2)}) copy-start(f32[1,7,8192]{2,0,1:T(1,128)} %param.10) | copy-start | bytes 688132
  0.0 61.6 %copy-start.5 = (f32[1,2,8192]{2,1,0:T(2,128)S(1)}, f32[1,2,8192]{2,1,0:T(2,128)}, u32[]{:S(2)}) copy-start(f32[1,2,8192]{2,1,0:T(2,128)} %gain_ref.7) | copy-start | bytes 196612
  1.7 110.2 %collective-permute-start.3 = (bf16[128,6144]{1,0:T(8,128)(2,1)S(1)}, bf16[128,6144]{1,0:T(8,128)(2,1)S(1)}, u32[]{:S(2)}, u32[]{:S(2)}) collective-permute-start(bf16[128,6144]{1,0:T(8,128)(2,1)S(1)} %slice.11), channel_id=1, source_target_pairs={{0,1},{1,2},{2,3},{3,4},{4,5},{5,6},{6,7},{7,8},{8,9},{9,10},{10,1... | collective-permute-start | bytes 4718600 | tf_op jit(solution)/shard_map/ppermute | solution.py:278
  6.1 128.8 %collective-permute-start = (bf16[128,2048]{1,0:T(8,128)(2,1)}, bf16[128,2048]{1,0:T(8,128)(2,1)S(1)}, u32[]{:S(2)}, u32[]{:S(2)}) collective-permute-start(bf16[128,2048]{1,0:T(8,128)(2,1)} %slice.9), channel_id=1, source_target_pairs={{0,1},{1,2},{2,3},{3,4},{4,5},{5,6},{6,7},{7,8},{8,9},{9,10},{10,1... | collective-permute-start | bytes 1572872 | tf_op jit(solution)/shard_map/ppermute | solution.py:278
  9.7 68.3 %copy-start.3 = (bf16[256,256]{1,0:T(8,128)(2,1)S(1)}, bf16[256,256]{1,0:T(8,128)(2,1)}, u32[]{:S(2)}) copy-start(bf16[256,256]{1,0:T(8,128)(2,1)} %constant.4.clone.forward_ref) | copy-start | bytes 393220
  9.7 68.2 %copy-start.6 = (bf16[1,128,512]{2,1,0:T(8,128)(2,1)S(1)}, bf16[1,128,512]{2,1,0:T(8,128)(2,1)}, u32[]{:S(2)}) copy-start(bf16[1,128,512]{2,1,0:T(8,128)(2,1)} %param.11) | copy-start | bytes 393220
  9.7 51.9 %collective-permute-start.1 = (bf16[16,8192]{1,0:T(8,128)(2,1)S(1)}, bf16[16,8192]{1,0:T(8,128)(2,1)S(1)}, u32[]{:S(2)}, u32[]{:S(2)}) collective-permute-start(bf16[16,8192]{1,0:T(8,128)(2,1)S(1)} %slice.10), channel_id=1, source_target_pairs={{0,1},{1,2},{2,3},{3,4},{4,5},{5,6},{6,7},{7,8},{8,9},{9,10},{10,1... | collective-permute-start | bytes 786440 | tf_op jit(solution)/shard_map/ppermute | solution.py:278
  75.7 10.3 %copy-start.2 = (bf16[208,8192]{1,0:T(8,128)(2,1)S(1)}, bf16[208,8192]{1,0:T(8,128)(2,1)}, u32[]{:S(2)}) copy-start(bf16[208,8192]{1,0:T(8,128)(2,1)} %get-tuple-element.12.mid_ref) | copy-start | bytes 10223620
  75.7 10.3 %copy-start.4 = (bf16[256,256]{1,0:T(8,128)(2,1)S(1)}, bf16[256,256]{1,0:T(8,128)(2,1)}, u32[]{:S(2)}) copy-start(bf16[256,256]{1,0:T(8,128)(2,1)} %constant.5.clone.backward_ref) | copy-start | bytes 393220
  75.7 36.1 %collective-permute-start.2 = (f32[8,256]{1,0:T(8,128)S(1)}, f32[8,256]{1,0:T(8,128)S(1)}, u32[]{:S(2)}, u32[]{:S(2)}) collective-permute-start(f32[8,256]{1,0:T(8,128)S(1)} %get-tuple-element.11), channel_id=1, source_target_pairs={{0,1},{1,2},{2,3},{3,4},{4,5},{5,6},{6,7},{7,8},{8,9},{9,10},{10,1... | collective-permute-start | bytes 24584 | tf_op jit(solution)/shard_map/ppermute | solution.py:278
  84.1 1.9 %copy-start = (bf16[256,8192]{1,0:T(8,128)(2,1)}, bf16[256,8192]{1,0:T(8,128)(2,1)S(1)}, u32[]{:S(2)}) copy-start(bf16[256,8192]{1,0:T(8,128)(2,1)S(1)} %taps_transform.1.table_ref) | copy-start | bytes 12582916

commit v2 on v1

v2 whole, which is shorter than its diff:
```python
import functools

import jax
import jax.numpy as jnp
import numpy as np
from jax import lax
from jax.experimental import pallas as pl
from jax.experimental.pallas import tpu as pltpu
from jax.sharding import PartitionSpec as P

F32 = jnp.float32
BF16 = jnp.bfloat16
EDGE = 16
HALO = 144
REACH = 128
POINTS = 256
HEAD = 32
PAD = 8
LANES = 128
WIDE = 256
STEP = 16
EPS = 1e-06
EARLY = (6144, 2048)
LATE = ((0, 2048), (2048, 2048), (4096, 2048))
OWN_BLOCK = 1024
HALO_BLOCK = 512
TAIL_BLOCK = 1024
VMEM_LIMIT = 20 * 1024 * 1024


def transform_tables():
    k = np.arange(POINTS // 2)[:, None]
    n = np.arange(POINTS)[None, :]
    angle = np.pi * ((2 * k + 1) * n % (2 * POINTS)) / POINTS
    forward = np.concatenate([np.cos(angle), -np.sin(angle)], axis=0)
    backward = forward.T * (2.0 / POINTS)
    return jnp.asarray(forward, BF16), jnp.asarray(backward, BF16)


def params(vmem=VMEM_LIMIT):
    return pltpu.CompilerParams(vmem_limit_bytes=vmem)


def cost(micros):
    return pl.CostEstimate(
        flops=int(micros * 1e6), bytes_accessed=int(micros * 3.7e6), transcendentals=0
    )


def tap_rows(gain, feat_ref, lanes):
    return [
        [feat_ref[0, 0, j, i : i + 1, lanes] * gain for i in range(3)] for j in range(3)
    ]


def three_taps(scaled_ref, at, taps):
    summed = taps[0] * scaled_ref[pl.ds(at, STEP), :]
    for i in range(1, 3):
        summed = summed + taps[i] * scaled_ref[pl.ds(at - i, STEP), :]
    return summed


def se_filter(product_ref, at, taps):
    summed = taps[0] * product_ref[pl.ds(at, STEP), :]
    for i in range(1, len(taps)):
        summed = summed + taps[i] * product_ref[pl.ds(at - i, STEP), :]
    return summed


def to_row(column, width):
    rows = column.shape[0]
    on = lax.broadcasted_iota(jnp.int32, (rows, width), 0) == lax.broadcasted_iota(
        jnp.int32, (rows, width), 1
    )
    return jnp.sum(jnp.where(on, column, 0.0), axis=0, keepdims=True)


def to_column(row, start, rows):
    width = row.shape[1]
    on = lax.broadcasted_iota(jnp.int32, (rows, width), 0) + start == lax.broadcasted_iota(
        jnp.int32, (rows, width), 1
    )
    return jnp.sum(jnp.where(on, row, 0.0), axis=1, keepdims=True)


def first_block():
    return (lax.axis_index("section") == 0) & (lax.axis_index("ctx") == 0)


def taps_transform_kernel(taps_ref, forward_ref, out_ref, spread):
    groups, wide = spread.shape

    @pl.when(pl.program_id(0) == 0)
    def _():
        channel = lax.broadcasted_iota(jnp.int32, (groups, wide), 1)
        group = lax.broadcasted_iota(jnp.int32, (groups, wide), 0)
        inside = (channel >= group * 16) & (channel < group * 16 + 16)
        spread[...] = jnp.where(inside, 1.0, 0.0).astype(BF16)

    few = jnp.dot(
        forward_ref[...], taps_ref[...], preferred_element_type=F32
    ).astype(BF16)
    for at in range(0, wide, WIDE):
        out_ref[:, at : at + WIDE] = jnp.dot(
            few, spread[:, at : at + WIDE], preferred_element_type=F32
        ).astype(BF16)


def lanes_of(j):
    return pl.ds(pl.multiple_of(j * LANES, LANES), LANES)


def se_operator(
    read, rows, first_row, width, shown, gain_ref, feat_ref, se_ref,
    mid_ref, first_inv, square, scaled, product,
):
    tiles = width // LANES
    square[...] = jnp.zeros_like(square)

    def add_squares(j, carry):
        for at in range(0, rows, STEP):
            summed = square[at : at + STEP, :]
            for i in range(8):
                x = read(at, j * 8 + i)
                summed = summed + x * x
            square[at : at + STEP, :] = summed
        return carry

    lax.fori_loop(0, tiles // 8, add_squares, 0)
    first = lax.rsqrt(jnp.sum(square[...], axis=1, keepdims=True) / width + EPS)
    first_inv[...] = jnp.broadcast_to(first, first_inv.shape)
    if shown is not None:
        first_inv[0:EDGE, :] = first_inv[0:EDGE, :] * shown
    square[...] = jnp.zeros_like(square)
    scaled[0:PAD, :] = jnp.zeros((PAD, LANES), F32)
    product[0:PAD, :] = jnp.zeros((PAD, LANES), F32)

    def one_tile(j, carry):
        lanes = lanes_of(j)
        taps = tap_rows(gain_ref[0, 0:1, lanes], feat_ref, lanes)
        filter_taps = [se_ref[0, i : i + 1, lanes] for i in range(7)]
        for at in range(0, rows, STEP):
            x = read(at, j)
            scaled[PAD + at : PAD + at + STEP, :] = x * first_inv[at : at + STEP, :]
        for at in range(0, rows, STEP):
            k = three_taps(scaled, PAD + at, taps[1])
            v = three_taps(scaled, PAD + at, taps[2])
            product[PAD + at : PAD + at + STEP, :] = (k * v).astype(BF16).astype(F32)
        for at in range(first_row, rows, STEP):
            q = three_taps(scaled, PAD + at, taps[0])
            f = se_filter(product, PAD + at, filter_taps)
            result = (read(at, j) + q * f).astype(BF16)
            mid_ref[at - first_row : at - first_row + STEP, lanes] = result
            wide_result = result.astype(F32)
            square[at : at + STEP, :] += wide_result * wide_result
        return carry

    lax.fori_loop(0, tiles, one_tile, 0)
    second = lax.rsqrt(
        jnp.sum(square[first_row:, :], axis=1, keepdims=True) / width + EPS
    )
    return first, second


def own_se_kernel(
    tokens_ref, gain_ref, feat_ref, se_ref, late_feat_ref,
    mid_ref, inv_ref, *rest,
):
    rows, width = tokens_ref.shape
    tail_refs, scratch = rest[: len(LATE)], rest[len(LATE) :]
    scaled = scratch[2]

    def read(at, j):
        return tokens_ref[at : at + STEP, lanes_of(j)].astype(F32)

    first, second = se_operator(
        read, rows, EDGE, width, None, gain_ref, feat_ref, se_ref, mid_ref, *scratch
    )
    inv_ref[...] = jnp.broadcast_to(second, inv_ref.shape)
    lead = rows - HALO

    for (start, size), tail_ref in zip(LATE, tail_refs):

        def one_tail(j, carry, start=start, tail_ref=tail_ref):
            lanes = lanes_of(start // LANES + j)
            taps = tap_rows(gain_ref[0, 1:2, lanes], late_feat_ref, lanes)
            for at in range(0, HALO, STEP):
                own = lead - EDGE + at
                scaled[at : at + STEP, :] = (
                    mid_ref[own : own + STEP, lanes].astype(F32)
                    * inv_ref[own : own + STEP, :]
                )
            for at in range(HALO - REACH, HALO, STEP):
                k = three_taps(scaled, at, taps[1])
                v = three_taps(scaled, at, taps[2])
                to = at - (HALO - REACH)
                tail_ref[to : to + STEP, lanes_of(j)] = (k * v).astype(BF16)
            return carry

        lax.fori_loop(0, size // LANES, one_tail, 0)

    top = lax.broadcasted_iota(jnp.int32, (STEP, WIDE), 0) == 0
    for i, norms in enumerate((first[EDGE:], second)):
        left = to_row(norms, WIDE)
        for k in range(3):
            piece = left.astype(BF16).astype(F32)
            left = left - piece
            lanes = pl.ds((i * 3 + k) * WIDE, WIDE)
            rest_of = tail_refs[0][0:STEP, lanes].astype(F32)
            tail_refs[0][0:STEP, lanes] = jnp.where(top, piece, rest_of).astype(BF16)


def head_se_kernel(
    tokens_ref, early_ref, gain_ref, feat_ref, se_ref,
    mid_ref, inv_ref,
    *scratch,
):
    width = tokens_ref.shape[1]
    shown = jnp.where(first_block(), 0.0, 1.0)

    span = EARLY[1] // LANES
    parts = EARLY[0] // EARLY[1]

    def read(at, j):
        if at < EDGE:
            part = lax.div(j, span)
            row = jnp.where(part < parts, HALO + EDGE * part, HALO - EDGE)
            column = j - span * part
            rows = pl.ds(pl.multiple_of(row + at, STEP), STEP)
            return early_ref[rows, lanes_of(column)].astype(F32)
        return tokens_ref[at - EDGE : at - EDGE + STEP, lanes_of(j)].astype(F32)

    _, second = se_operator(
        read, HEAD, 0, width, shown, gain_ref, feat_ref, se_ref, mid_ref, *scratch
    )
    inv_ref[...] = jnp.broadcast_to(second, inv_ref.shape)
    inv_ref[0:EDGE, :] = inv_ref[0:EDGE, :] * shown


def multiply_spectra(spectrum, taps_ref, out_ref, lanes):
    half = POINTS // 2
    for at in range(0, half, STEP):
        a, b = spectrum[at : at + STEP], spectrum[half + at : half + at + STEP]
        c = taps_ref[at : at + STEP, lanes].astype(F32)
        d = taps_ref[half + at : half + at + STEP, lanes].astype(F32)
        out_ref[at : at + STEP, lanes] = (a * c - b * d).astype(BF16)
        out_ref[half + at : half + at + STEP, lanes] = (a * d + b * c).astype(BF16)


def staggered(count, *stages):
    for step in range(count + len(stages) - 1):
        for i, stage in enumerate(stages):
            if 0 <= step - i < count:
                stage(step - i)


def own_mr_kernel(
    head_ref, mid_ref, head_inv_ref, inv_ref, gain_ref, feat_ref, table_ref,
    forward_ref, backward_ref,
    out_ref, base_ref, gate_ref,
    scaled, product, late_gate, spectrum, late_spectrum,
):
    total = HEAD + mid_ref.shape[0]
    rows = total - EDGE

    def read(at, lanes):
        if at < HEAD:
            return head_ref[at : at + STEP, lanes].astype(F32)
        return mid_ref[at - HEAD : at - HEAD + STEP, lanes].astype(F32)

    def inverse(at):
        if at < HEAD:
            return head_inv_ref[at : at + STEP, :]
        return inv_ref[at - HEAD : at - HEAD + STEP, :]

    def streams(tile):
        for half in range(WIDE // LANES):
            lanes = pl.ds(tile * WIDE + half * LANES, LANES)
            column = scaled.at[tile * 2 + half]
            taps = tap_rows(gain_ref[0, 1:2, lanes], feat_ref, lanes)
            for at in range(0, total, STEP):
                column[at : at + STEP, :] = read(at, lanes) * inverse(at)
            for at in range(0, rows, STEP):
                k = three_taps(column, EDGE + at, taps[1])
                v = three_taps(column, EDGE + at, taps[2])
                w = (k * v).astype(BF16)
                product[at : at + STEP, lanes] = w
                q = three_taps(column, EDGE + at, taps[0])
                if at < REACH:
                    gate_ref[at : at + STEP, lanes] = q
                else:
                    late_gate[at - REACH : at - REACH + STEP, lanes] = q

    def spectra(tile):
        lanes = pl.ds(tile * WIDE, WIDE)
        early = jnp.dot(
            forward_ref[:, REACH:], product[0:REACH, lanes], preferred_element_type=F32
        )
        multiply_spectra(early, table_ref, spectrum, lanes)
        late = jnp.dot(
            forward_ref[:, 0:rows], product[:, lanes], preferred_element_type=F32
        )
        multiply_spectra(late, table_ref, late_spectrum, lanes)

    def results(tile):
        lanes = pl.ds(tile * WIDE, WIDE)
        first = jnp.dot(
            backward_ref[REACH:, :], spectrum[:, lanes], preferred_element_type=F32
        )
        for at in range(0, REACH, STEP):
            base_ref[at : at + STEP, lanes] = (
                read(EDGE + at, lanes)
                + gate_ref[at : at + STEP, lanes] * first[at : at + STEP]
            )
        last = jnp.dot(
            backward_ref[REACH:rows, :],
            late_spectrum[:, lanes],
            preferred_element_type=F32,
        )
        for at in range(0, rows - REACH, STEP):
            out_ref[at : at + STEP, lanes] = (
                read(EDGE + REACH + at, lanes)
                + late_gate[at : at + STEP, lanes] * last[at : at + STEP]
            ).astype(BF16)

    staggered(mid_ref.shape[1] // WIDE, streams, spectra, results)


def halo_kernel(
    main_ref, stat_ref, gain_ref, feat_first_ref, se_ref, feat_ref, table_ref,
    forward_ref, backward_ref, base_ref, gate_ref, held_ref,
    out_ref,
    first_inv, second_inv, scaled, se_product, again, product, spectrum,
    *, start,
):
    del held_ref
    columns = scaled.shape[0]

    @pl.when(pl.program_id(0) == 0)
    def _():
        shown = jnp.where(first_block(), 0.0, 1.0)
        for i, inverse in enumerate((first_inv, second_inv)):
            row = jnp.zeros((1, WIDE), F32)
            for k in range(3):
                lanes = pl.ds((i * 3 + k) * WIDE, WIDE)
                row = row + stat_ref[0:STEP, lanes].astype(F32)[0:1]
            column = to_column(row * shown, start, HALO)
            inverse[...] = jnp.broadcast_to(column, inverse.shape)
        scaled[:, 0:PAD, :] = jnp.zeros((columns, PAD, LANES), F32)
        se_product[:, 0:PAD, :] = jnp.zeros((columns, PAD, LANES), F32)

    def read(at, lanes):
        return main_ref[at : at + STEP, lanes].astype(F32)

    def streams(tile):
        for half in range(WIDE // LANES):
            lanes = pl.ds(tile * WIDE + half * LANES, LANES)
            column = scaled.at[tile * 2 + half]
            se_column = se_product.at[tile * 2 + half]
            late_column = again.at[tile * 2 + half]
            taps = tap_rows(gain_ref[0, 0:1, lanes], feat_first_ref, lanes)
            filter_taps = [se_ref[0, i : i + 1, lanes] for i in range(7)]
            late_taps = tap_rows(gain_ref[0, 1:2, lanes], feat_ref, lanes)
            for at in range(0, HALO, STEP):
                column[PAD + at : PAD + at + STEP, :] = (
                    read(at, lanes) * first_inv[at : at + STEP, :]
                )
            for at in range(0, HALO, STEP):
                k = three_taps(column, PAD + at, taps[1])
                v = three_taps(column, PAD + at, taps[2])
                se_column[PAD + at : PAD + at + STEP, :] = (
                    (k * v).astype(BF16).astype(F32)
                )
            for at in range(0, HALO, STEP):
                q = three_taps(column, PAD + at, taps[0])
                f = se_filter(se_column, PAD + at, filter_taps)
                result = (read(at, lanes) + q * f).astype(BF16).astype(F32)
                late_column[at : at + STEP, :] = result * second_inv[at : at + STEP, :]
            for at in range(HALO - REACH, HALO, STEP):
                k = three_taps(late_column, at, late_taps[1])
                v = three_taps(late_column, at, late_taps[2])
                to = at - (HALO - REACH)
                product[to : to + STEP, lanes] = (k * v).astype(BF16)

    def spectra(tile):
        halo_spectra(tile, product, forward_ref, table_ref, spectrum)

    def results(tile):
        halo_results(tile, spectrum, backward_ref, base_ref, gate_ref, out_ref)

    staggered(main_ref.shape[1] // WIDE, streams, spectra, results)


def halo_spectra(tile, product, forward_ref, table_ref, spectrum):
    lanes = pl.ds(tile * WIDE, WIDE)
    seen = jnp.dot(
        forward_ref[:, 0:REACH], product[:, lanes], preferred_element_type=F32
    )
    multiply_spectra(seen, table_ref, spectrum, lanes)


def halo_results(tile, spectrum, backward_ref, base_ref, gate_ref, out_ref):
    lanes = pl.ds(tile * WIDE, WIDE)
    carried = jnp.dot(
        backward_ref[REACH:, :], spectrum[:, lanes], preferred_element_type=F32
    )
    for at in range(0, REACH, STEP):
        out_ref[at : at + STEP, lanes] = (
            base_ref[at : at + STEP, lanes]
            + gate_ref[at : at + STEP, lanes] * carried[at : at + STEP]
        ).astype(BF16)


def tail_kernel(
    tail_ref, shown_table_ref, forward_ref, backward_ref, base_ref, gate_ref, held_ref,
    out_ref,
    product, spectrum,
):
    del held_ref
    shown = jnp.where(first_block(), 0.0, 1.0)
    block = tail_ref.shape[1]

    def arrived(tile):
        lanes = pl.ds(tile * WIDE, WIDE)
        for at in range(0, REACH, STEP):
            w = tail_ref[at : at + STEP, lanes].astype(F32) * shown
            if at == 0:
                w = jnp.where(
                    lax.broadcasted_iota(jnp.int32, w.shape, 0) == 0, 0.0, w
                )
            product[at : at + STEP, lanes] = w.astype(BF16)

    def spectra(tile):
        halo_spectra(tile, product, forward_ref, shown_table_ref, spectrum)

    def results(tile):
        halo_results(tile, spectrum, backward_ref, base_ref, gate_ref, out_ref)

    staggered(block // WIDE, arrived, spectra, results)


def whole(array):
    return pl.BlockSpec(array.shape, lambda *_: (0,) * array.ndim)


def on_device(tokens, norm_gain, feat_taps, se_taps, mr_taps):
    rows, width = tokens.shape
    total = rows + EDGE
    forward, backward = transform_tables()
    length = lax.axis_size(("section", "ctx"))

    def from_behind(x):
        pairs = [(i, (i + 1) % length) for i in range(length)]
        return lax.ppermute(x, ("section", "ctx"), pairs)

    start, size = EARLY
    early = from_behind(
        jnp.concatenate(
            [tokens[rows - HALO :, start:]]
            + [tokens[rows - EDGE :, i : i + size] for i in range(0, start, size)],
            axis=0,
        )
    )

    groups = 2048 // 16
    table = pl.pallas_call(
        taps_transform_kernel,
        grid=(width // 2048,),
        in_specs=[
            pl.BlockSpec((REACH, groups), lambda j: (0, j)),
            pl.BlockSpec((POINTS, REACH), lambda j: (0, 0)),
        ],
        out_specs=pl.BlockSpec((POINTS, 2048), lambda j: (0, j)),
        out_shape=jax.ShapeDtypeStruct((POINTS, width), BF16),
        scratch_shapes=[pltpu.VMEM((groups, 2048), BF16)],
        compiler_params=params(),
        cost_estimate=cost(2.5),
        name="taps_transform",
    )(mr_taps[0], forward)

    se_specs = [
        whole(norm_gain),
        pl.BlockSpec((1, 1, 3, 3, width), lambda i: (0, 0, 0, 0, 0)),
        whole(se_taps),
    ]

    def se_scratch(height):
        return [
            pltpu.VMEM((height, LANES), F32),
            pltpu.VMEM((height, LANES), F32),
            pltpu.VMEM((PAD + height, LANES), F32),
            pltpu.VMEM((PAD + height, LANES), F32),
        ]

    def all_of(*shape):
        return pl.BlockSpec(shape, lambda *_: (0,) * len(shape))

    mid_rows = rows - EDGE
    mid, inv, *tails = pl.pallas_call(
        own_se_kernel,
        grid=(1,),
        in_specs=[
            whole(tokens),
            *se_specs,
            pl.BlockSpec((1, 1, 3, 3, width), lambda i: (0, 1, 0, 0, 0)),
        ],
        out_specs=[all_of(mid_rows, width), all_of(mid_rows, LANES)]
        + [all_of(REACH, size) for _, size in LATE],
        out_shape=[
            jax.ShapeDtypeStruct((mid_rows, width), BF16),
            jax.ShapeDtypeStruct((mid_rows, LANES), F32),
        ]
        + [jax.ShapeDtypeStruct((REACH, size), BF16) for _, size in LATE],
        scratch_shapes=se_scratch(rows),
        compiler_params=params(),
        cost_estimate=cost(14),
        name="own_se",
    )(tokens, norm_gain, feat_taps, se_taps, feat_taps)
    tails = [from_behind(tail) for tail in tails]

    head, head_inv = pl.pallas_call(
        head_se_kernel,
        grid=(1,),
        in_specs=[all_of(EDGE, width), whole(early), *se_specs],
        out_specs=[all_of(HEAD, width), all_of(HEAD, LANES)],
        out_shape=[
            jax.ShapeDtypeStruct((HEAD, width), BF16),
            jax.ShapeDtypeStruct((HEAD, LANES), F32),
        ],
        scratch_shapes=se_scratch(HEAD),
        compiler_params=params(),
        cost_estimate=cost(3),
        name="head_se",
    )(tokens, early, norm_gain, feat_taps, se_taps)

    def feat_spec(block, which, first):
        return pl.BlockSpec((1, 1, 3, 3, block), lambda j: (0, which, 0, 0, first + j))

    def columns(height, block, first=0, row=0):
        return pl.BlockSpec((height, block), lambda j: (row, first + j))

    block = OWN_BLOCK
    out, base, gate = pl.pallas_call(
        own_mr_kernel,
        grid=(width // block,),
        in_specs=[
            columns(HEAD, block),
            columns(mid_rows, block),
            whole(head_inv),
            whole(inv),
            pl.BlockSpec((1, 2, block), lambda j: (0, 0, j)),
            feat_spec(block, 1, 0),
            columns(POINTS, block),
            whole(forward),
            whole(backward),
        ],
        out_specs=[
            columns(rows - REACH, block, 0, REACH // (rows - REACH)),
            columns(REACH, block),
            columns(REACH, block),
        ],
        out_shape=[
            jax.ShapeDtypeStruct((rows, width), BF16),
            jax.ShapeDtypeStruct((REACH, width), F32),
            jax.ShapeDtypeStruct((REACH, width), F32),
        ],
        scratch_shapes=[
            pltpu.VMEM((block // LANES, rows + EDGE, LANES), F32),
            pltpu.VMEM((rows, block), BF16),
            pltpu.VMEM((rows - REACH, block), F32),
            pltpu.VMEM((POINTS, block), BF16),
            pltpu.VMEM((POINTS, block), BF16),
        ],
        compiler_params=params(),
        cost_estimate=cost(12),
        name="own_mr",
    )(head, mid, head_inv, inv, norm_gain, feat_taps, table, forward, backward)

    block = HALO_BLOCK
    first = start // block
    out = pl.pallas_call(
        functools.partial(halo_kernel, start=mid_rows - HALO),
        grid=(size // block,),
        in_specs=[
            columns(HALO, block),
            all_of(STEP, 6 * WIDE),
            pl.BlockSpec((1, 2, block), lambda j: (0, 0, first + j)),
            feat_spec(block, 0, first),
            pl.BlockSpec((1, 7, block), lambda j: (0, 0, first + j)),
            feat_spec(block, 1, first),
            columns(POINTS, block, first),
            whole(forward),
            whole(backward),
            columns(REACH, block, first),
            columns(REACH, block, first),
            pl.BlockSpec(memory_space=pl.ANY),
        ],
        out_specs=columns(REACH, block, first),
        out_shape=jax.ShapeDtypeStruct((rows, width), BF16),
        input_output_aliases={11: 0},
        scratch_shapes=[
            pltpu.VMEM((HALO, LANES), F32),
            pltpu.VMEM((HALO, LANES), F32),
            pltpu.VMEM((block // LANES, PAD + HALO, LANES), F32),
            pltpu.VMEM((block // LANES, PAD + HALO, LANES), F32),
            pltpu.VMEM((block // LANES, HALO, LANES), F32),
            pltpu.VMEM((REACH, block), BF16),
            pltpu.VMEM((POINTS, block), BF16),
        ],
        compiler_params=params(),
        cost_estimate=cost(6),
        name="halo",
    )(
        early, tails[0], norm_gain, feat_taps, se_taps, feat_taps, table,
        forward, backward, base, gate, out,
    )

    block = TAIL_BLOCK
    for (start, size), tail in zip(LATE, tails):
        out = pl.pallas_call(
            tail_kernel,
            grid=(size // block,),
            in_specs=[
                columns(REACH, block),
                columns(POINTS, block, start // block),
                whole(forward),
                whole(backward),
                columns(REACH, block, start // block),
                columns(REACH, block, start // block),
                pl.BlockSpec(memory_space=pl.ANY),
            ],
            out_specs=columns(REACH, block, start // block),
            out_shape=jax.ShapeDtypeStruct((rows, width), BF16),
            input_output_aliases={6: 0},
            scratch_shapes=[
                pltpu.VMEM((REACH, block), BF16),
                pltpu.VMEM((POINTS, block), BF16),
            ],
            compiler_params=params(),
            cost_estimate=cost(3),
        name="tail",
        )(tail, table, forward, backward, base, gate, out)
    return out


def solution(mesh):
    placed = (P(("section", "ctx"), None), P(), P(), P(), P())
    return jax.shard_map(
        on_device,
        mesh=mesh,
        in_specs=placed,
        out_specs=P(("section", "ctx"), None),
        check_vma=False,
    )
```

time: 145 us -> 64.3 us (0.44)
  the two profiles are of different devices: /device:TPU:7 before, /device:TPU:1 now
where the time goes in v2:
time: 64.3 us; the launch traced here: 64.2 us
  Pallas kernels  44.1 us (69%)
  waiting for transfers between devices  9.5 us (15%)
  starting transfers between devices  5.67 us (9%)
  local copies, waits for them, and re-layouts  4.79 us (7%)
    pallas_call x1, Pallas kernels, on_device(): pl.pallas_call(own_se_kernel, grid=(1,), in_specs=[whole(tokens), *se_spe...  13 us
    pallas_call x1, Pallas kernels, on_device(): pl.pallas_call(own_mr_kernel, grid=(width // block,), in_specs=[columns(H...  11.9 us
    ppermute x4, waiting for transfers between devices, from_behind(): return lax.ppermute(x, ('section', 'ctx'), pairs)  9.5 us
    pallas_call x3, Pallas kernels, on_device(): pl.pallas_call(tail_kernel, grid=(size // block,), in_specs=[columns(REAC...  7.31 us
    ppermute x4, starting transfers between devices, from_behind(): return lax.ppermute(x, ('section', 'ctx'), pairs)  5.67 us
    pallas_call x1, Pallas kernels, on_device(): pl.pallas_call(functools.partial(halo_kernel, start=mid_rows - HALO), gri...  5.44 us
    pallas_call x1, Pallas kernels, on_device(): pl.pallas_call(head_se_kernel, grid=(1,), in_specs=[all_of(EDGE, width),...  3.83 us
    pallas_call x1, Pallas kernels, on_device(): pl.pallas_call(taps_transform_kernel, grid=(width // 2048,), in_specs=[pl...  2.66 us
  transfers between devices with their start and end apart: 4, of which 3 were waited for; matrix products, arithmetic and copies ran while one was open for 4% of the time, Pallas kernels for 65%

profile of v2, /device:TPU:1, one launch (start us, length us, event | category | flops | bytes accessed | tf_op | source)
XLA Modules:
  0.0 64.2 jit_solution(14972490990681250616)
XLA Ops:
  0.0 1.1 %fusion = (bf16[16,2048]{1,0:T(8,128)(2,1)S(1)}, bf16[16,2048]{1,0:T(8,128)(2,1)S(1)}, bf16[16,2048]{1,0:T(8,128)(2,1)S(1)}) fusion(bf16[192,8192]{1,0:T(8,128)(2,1)} %tokens_ref.3), kind=kLoop, calls=%fused_computation.1 | loop fusion | bytes 393216 | tf_op jit(solution)/shard_map/slice | solution.py:460
  1.1 1.1 %slice.12 = bf16[144,2048]{1,0:T(8,128)(2,1)S(1)} slice(bf16[192,8192]{1,0:T(8,128)(2,1)} %tokens_ref.3), slice={[48:192], [6144:8192]} | slice | bytes 1179648 | tf_op jit(solution)/shard_map/slice | solution.py:459
  2.2 0.1 pad_maximum_fusion
  2.3 2.5 %collective-permute-start.1 = (bf16[192,2048]{1,0:T(8,128)(2,1)S(1)}, bf16[192,2048]{1,0:T(8,128)(2,1)S(1)}, u32[]{:S(2)}, u32[]{:S(2)}) collective-permute-start(bf16[192,2048]{1,0:T(8,128)(2,1)S(1)} %pad_maximum_fusion), channel_id=1, source_target_pairs={{0,1},{1,2},{2,3},{3,4},{4,5},{5,6},{6,7},{7,8},{8,9},{9,10},{10,1... | collective-permute-start | bytes 2359304 | tf_op jit(solution)/shard_map/ppermute | solution.py:454
  4.8 1.1 %copy.13.se_ref = f32[1,7,8192]{2,1,0:T(8,128)S(1)} copy(f32[1,7,8192]{2,0,1:T(1,128)} %param.10) | data formatting | bytes 458752 | tf_op args[3]
  5.9 0.0 copy-start.1
  5.9 0.0 copy-start.4
  5.9 1.5 %copy.12.feat_ref.late_feat_ref.feat_first_ref = f32[1,2,3,3,8192]{4,3,2,1,0:T(4,128)S(1)} copy(f32[1,2,3,3,8192]{4,1,3,2,0:T(2,128)} %param.9) | data formatting | bytes 1179648 | tf_op args[2]
  7.4 13.0 %own_se.1 = (bf16[176,8192]{1,0:T(8,128)(2,1)S(1)}, f32[176,128]{1,0:T(8,128)S(1)}, bf16[128,2048]{1,0:T(8,128)(2,1)S(1)}, bf16[128,2048]{1,0:T(8,128)(2,1)S(1)}, bf16[128,2048]{1,0:T(8,128)(2,1)S(1)}) custom-call(bf16[192,8192]{1,0:T(8,128)(2,1)S(1)} %copy-done, f32[1,2,8192]{2,1,0:T(2,128)S(1)} %copy-done.3, ...), custom_call_target="tpu_custom_call" | custom-call | flops 14000000 | bytes 51800000 | tf_op jit(solution)/shard_map/own_se/pallas_call | solution.py:499
  20.4 1.7 %collective-permute-start.3 = (bf16[128,2048]{1,0:T(8,128)(2,1)S(1)}, bf16[128,2048]{1,0:T(8,128)(2,1)S(1)}, u32[]{:S(2)}, u32[]{:S(2)}) collective-permute-start(bf16[128,2048]{1,0:T(8,128)(2,1)S(1)} %get-tuple-element.23), channel_id=1, source_target_pairs={{0,1},{1,2},{2,3},{3,4},{4,5},{5,6},{6,7},{7,8},{8,9},{9,10},{10,1... | collective-permute-start | bytes 1572872 | tf_op jit(solution)/shard_map/ppermute | solution.py:454
  22.1 1.3 %collective-permute-start.2 = (bf16[128,2048]{1,0:T(8,128)(2,1)S(1)}, bf16[128,2048]{1,0:T(8,128)(2,1)S(1)}, u32[]{:S(2)}, u32[]{:S(2)}) collective-permute-start(bf16[128,2048]{1,0:T(8,128)(2,1)S(1)} %get-tuple-element.22), channel_id=1, source_target_pairs={{0,1},{1,2},{2,3},{3,4},{4,5},{5,6},{6,7},{7,8},{8,9},{9,10},{10,1... | collective-permute-start | bytes 1572872 | tf_op jit(solution)/shard_map/ppermute | solution.py:454
  23.5 0.1 collective-permute-start
  23.6 2.7 %taps_transform.1.table_ref.shown_table_ref = bf16[256,8192]{1,0:T(8,128)(2,1)S(1)} custom-call(bf16[128,512]{1,0:T(8,128)(2,1)S(1)} %bitcast.1, bf16[256,256]{1,0:T(8,128)(2,1)S(1)} %copy-done.1), custom_call_target="tpu_custom_call" | custom-call | flops 2500000 | bytes 9250000 | tf_op jit(solution)/shard_map/taps_transform/pallas_call | solution.py:466
  26.2 0.0 copy-start.2
  26.2 1.8 %collective-permute-done.1.early_ref.main_ref = bf16[192,2048]{1,0:T(8,128)(2,1)S(1)} collective-permute-done((bf16[192,2048]{1,0:T(8,128)(2,1)S(1)}, bf16[192,2048]{1,0:T(8,128)(2,1)S(1)}, u32[]{:S(2)}, u32[]{:S(2)}) %collective-permute-start.1) | collective-permute-done | bytes 786464 | tf_op jit(solution)/shard_map/ppermute | solution.py:454
  28.0 3.8 %head_se.1 = (bf16[32,8192]{1,0:T(8,128)(2,1)S(1)}, f32[32,128]{1,0:T(8,128)S(1)}) custom-call(bf16[192,8192]{1,0:T(8,128)(2,1)S(1)} %copy-done, bf16[192,2048]{1,0:T(8,128)(2,1)S(1)} %collective-permute-done.1.early_ref.main_ref, f32[1,2,8192]{2,1,0:T(2,128)S(1)} %copy-done.3, f32[1,2,3,3,8192]{4,3,2,1,0:T(4,128)S(1)} %copy.12.feat_ref.late_feat_ref.feat_first_ref, ...), custom_call_target="tpu_custom_call" | custom-call | flops 3000000 | bytes 11100000 | tf_op jit(solution)/shard_map/head_se/pallas_call | solution.py:521
  31.9 11.9 %own_mr.1 = (bf16[192,8192]{1,0:T(8,128)(2,1)}, f32[128,8192]{1,0:T(8,128)S(1)}, f32[128,8192]{1,0:T(8,128)S(1)}) custom-call(bf16[32,8192]{1,0:T(8,128)(2,1)S(1)} %get-tuple-element.16.head_ref, bf16[176,8192]{1,0:T(8,128)(2,1)S(1)} %get-tuple-element.17.mid_ref, f32[32,128]{1,0:T(8,128)S(1)} %get-tuple-element.18.head_inv_ref, ...), custom_call_target="tpu_custom_call" | custom-call | flops 12000000 | bytes 44400000 | tf_op jit(solution)/shard_map/own_mr/pallas_call | solution.py:543
  43.7 6.8 %collective-permute-done.3.stat_ref.tail_ref = bf16[128,2048]{1,0:T(8,128)(2,1)S(1)} collective-permute-done((bf16[128,2048]{1,0:T(8,128)(2,1)S(1)}, bf16[128,2048]{1,0:T(8,128)(2,1)S(1)}, u32[]{:S(2)}, u32[]{:S(2)}) %collective-permute-start.3) | collective-permute-done | bytes 524320 | tf_op jit(solution)/shard_map/ppermute | solution.py:454
  50.5 5.4 %halo.1.held_ref = bf16[192,8192]{1,0:T(8,128)(2,1)} custom-call(bf16[192,2048]{1,0:T(8,128)(2,1)S(1)} %collective-permute-done.1.early_ref.main_ref, bf16[128,2048]{1,0:T(8,128)(2,1)S(1)} %collective-permute-done.3.stat_ref.tail_ref, f32[1,2,8192]{2,1,0:T(2,128)S(1)} %copy-done.3, ...), custom_call_target="tpu_custom_call", output_to_operand_aliasing={{}: (11, {})} | custom-call | flops 6000000 | bytes 22200000 | tf_op jit(solution)/shard_map/halo/pallas_call | solution.py:581
  55.9 2.4 %tail.3.held_ref = bf16[192,8192]{1,0:T(8,128)(2,1)} custom-call(bf16[128,2048]{1,0:T(8,128)(2,1)S(1)} %collective-permute-done.3.stat_ref.tail_ref, bf16[256,8192]{1,0:T(8,128)(2,1)S(1)} %taps_transform.1.table_ref.shown_table_ref, bf16[256,256]{1,0:T(8,128)(2,1)S(1)} %copy-done.1, bf16[256,256]{1,0:T(8,128)(2,1)S(1)} %copy-done.2, ...), custom_call_target="tpu_custom_call", output_to_operand_aliasing={{}: (6, {})} | custom-call | flops 3000000 | bytes 11100000 | tf_op jit(solution)/shard_map/tail/pallas_call | solution.py:620
  58.4 0.0 collective-permute-done.2.tail_ref
  58.4 2.4 %tail.4.held_ref = bf16[192,8192]{1,0:T(8,128)(2,1)} custom-call(bf16[128,2048]{1,0:T(8,128)(2,1)S(1)} %collective-permute-done.2.tail_ref, bf16[256,8192]{1,0:T(8,128)(2,1)S(1)} %taps_transform.1.table_ref.shown_table_ref, bf16[256,256]{1,0:T(8,128)(2,1)S(1)} %copy-done.1, bf16[256,256]{1,0:T(8,128)(2,1)S(1)} %copy-done.2, ...), custom_call_target="tpu_custom_call", output_to_operand_aliasing={{}: (6, {})} | custom-call | flops 3000000 | bytes 11100000 | tf_op jit(solution)/shard_map/tail/pallas_call | solution.py:620
  60.8 0.9 %collective-permute-done.tail_ref = bf16[128,2048]{1,0:T(8,128)(2,1)S(1)} collective-permute-done((bf16[128,2048]{1,0:T(8,128)(2,1)S(1)}, bf16[128,2048]{1,0:T(8,128)(2,1)S(1)}, u32[]{:S(2)}, u32[]{:S(2)}) %collective-permute-start) | collective-permute-done | bytes 524320 | tf_op jit(solution)/shard_map/ppermute | solution.py:454
  61.7 2.4 %tail.5 = bf16[192,8192]{1,0:T(8,128)(2,1)} custom-call(bf16[128,2048]{1,0:T(8,128)(2,1)S(1)} %collective-permute-done.tail_ref, bf16[256,8192]{1,0:T(8,128)(2,1)S(1)} %taps_transform.1.table_ref.shown_table_ref, bf16[256,256]{1,0:T(8,128)(2,1)S(1)} %copy-done.1, bf16[256,256]{1,0:T(8,128)(2,1)S(1)} %copy-done.2, ...), custom_call_target="tpu_custom_call", output_to_operand_aliasing={{}: (6, {})} | custom-call | flops 3000000 | bytes 11100000 | tf_op jit(solution)/shard_map/tail/pallas_call | solution.py:620
  (7 shorter events, 0.0 us)
Async XLA Ops:
  0.0 7.4 %copy-start = (bf16[192,8192]{1,0:T(8,128)(2,1)S(1)}, bf16[192,8192]{1,0:T(8,128)(2,1)}, u32[]{:S(2)}) copy-start(bf16[192,8192]{1,0:T(8,128)(2,1)} %tokens_ref.3) | copy-start | bytes 9437188
  0.0 7.4 %copy-start.3 = (f32[1,2,8192]{2,1,0:T(2,128)S(1)}, f32[1,2,8192]{2,1,0:T(2,128)}, u32[]{:S(2)}) copy-start(f32[1,2,8192]{2,1,0:T(2,128)} %gain_ref.7) | copy-start | bytes 196612
  2.3 25.8 %collective-permute-start.1 = (bf16[192,2048]{1,0:T(8,128)(2,1)S(1)}, bf16[192,2048]{1,0:T(8,128)(2,1)S(1)}, u32[]{:S(2)}, u32[]{:S(2)}) collective-permute-start(bf16[192,2048]{1,0:T(8,128)(2,1)S(1)} %pad_maximum_fusion), channel_id=1, source_target_pairs={{0,1},{1,2},{2,3},{3,4},{4,5},{5,6},{6,7},{7,8},{8,9},{9,10},{10,1... | collective-permute-start | bytes 2359304 | tf_op jit(solution)/shard_map/ppermute | solution.py:454
  5.9 17.7 %copy-start.1 = (bf16[256,256]{1,0:T(8,128)(2,1)S(1)}, bf16[256,256]{1,0:T(8,128)(2,1)}, u32[]{:S(2)}) copy-start(bf16[256,256]{1,0:T(8,128)(2,1)} %constant.4.clone.forward_ref) | copy-start | bytes 393220
  5.9 17.7 %copy-start.4 = (bf16[1,128,512]{2,1,0:T(8,128)(2,1)S(1)}, bf16[1,128,512]{2,1,0:T(8,128)(2,1)}, u32[]{:S(2)}) copy-start(bf16[1,128,512]{2,1,0:T(8,128)(2,1)} %param.11) | copy-start | bytes 393220
  20.4 30.1 %collective-permute-start.3 = (bf16[128,2048]{1,0:T(8,128)(2,1)S(1)}, bf16[128,2048]{1,0:T(8,128)(2,1)S(1)}, u32[]{:S(2)}, u32[]{:S(2)}) collective-permute-start(bf16[128,2048]{1,0:T(8,128)(2,1)S(1)} %get-tuple-element.23), channel_id=1, source_target_pairs={{0,1},{1,2},{2,3},{3,4},{4,5},{5,6},{6,7},{7,8},{8,9},{9,10},{10,1... | collective-permute-start | bytes 1572872 | tf_op jit(solution)/shard_map/ppermute | solution.py:454
  22.1 36.3 %collective-permute-start.2 = (bf16[128,2048]{1,0:T(8,128)(2,1)S(1)}, bf16[128,2048]{1,0:T(8,128)(2,1)S(1)}, u32[]{:S(2)}, u32[]{:S(2)}) collective-permute-start(bf16[128,2048]{1,0:T(8,128)(2,1)S(1)} %get-tuple-element.22), channel_id=1, source_target_pairs={{0,1},{1,2},{2,3},{3,4},{4,5},{5,6},{6,7},{7,8},{8,9},{9,10},{10,1... | collective-permute-start | bytes 1572872 | tf_op jit(solution)/shard_map/ppermute | solution.py:454
  23.5 38.3 %collective-permute-start = (bf16[128,2048]{1,0:T(8,128)(2,1)S(1)}, bf16[128,2048]{1,0:T(8,128)(2,1)S(1)}, u32[]{:S(2)}, u32[]{:S(2)}) collective-permute-start(bf16[128,2048]{1,0:T(8,128)(2,1)S(1)} %get-tuple-element.15), channel_id=1, source_target_pairs={{0,1},{1,2},{2,3},{3,4},{4,5},{5,6},{6,7},{7,8},{8,9},{9,10},{10,1... | collective-permute-start | bytes 1572872 | tf_op jit(solution)/shard_map/ppermute | solution.py:454
  26.2 5.7 %copy-start.2 = (bf16[256,256]{1,0:T(8,128)(2,1)S(1)}, bf16[256,256]{1,0:T(8,128)(2,1)}, u32[]{:S(2)}) copy-start(bf16[256,256]{1,0:T(8,128)(2,1)} %constant.5.clone.backward_ref) | copy-start | bytes 393220

commit v3 on v2

--- a/solution.py
+++ b/solution.py
@@ -20,8 +20,11 @@
 WIDE = 256
 STEP = 16
 EPS = 1e-06
-EARLY = (6144, 2048)
+EARLY = (7168, 1024)
+ROUND = (6144, 1024)
 LATE = ((0, 2048), (2048, 2048), (4096, 2048))
+RING = 4
+PIECES = 2
 OWN_BLOCK = 1024
 HALO_BLOCK = 512
 TAIL_BLOCK = 1024
@@ -34,7 +37,8 @@
     angle = np.pi * ((2 * k + 1) * n % (2 * POINTS)) / POINTS
     forward = np.concatenate([np.cos(angle), -np.sin(angle)], axis=0)
     backward = forward.T * (2.0 / POINTS)
-    return jnp.asarray(forward, BF16), jnp.asarray(backward, BF16)
+    late = forward[:, :REACH] * (np.arange(REACH) > 0)
+    return tuple(jnp.asarray(table, BF16) for table in (forward, backward, late))
 
 
 def params(vmem=VMEM_LIMIT):
@@ -85,6 +89,25 @@
 
 def first_block():
     return (lax.axis_index("section") == 0) & (lax.axis_index("ctx") == 0)
+
+
+def gather_kernel(tokens_ref, early_ref, around_ref, done):
+    rows = tokens_ref.shape[0]
+    halo, edge = pl.ds(rows - HALO, HALO), pl.ds(rows - EDGE, EDGE)
+    start, size = EARLY
+    moves = [(tokens_ref.at[halo, pl.ds(*ROUND)], around_ref)]
+    moves.append((tokens_ref.at[halo, pl.ds(*EARLY)], early_ref.at[pl.ds(0, HALO), :]))
+    for i in range(start // size):
+        to = early_ref.at[pl.ds(HALO + EDGE * i, EDGE), :]
+        moves.append((tokens_ref.at[edge, pl.ds(i * size, size)], to))
+    copies = [
+        pltpu.make_async_copy(source, to, done.at[i])
+        for i, (source, to) in enumerate(moves)
+    ]
+    for copy in copies:
+        copy.start()
+    for copy in copies:
+        copy.wait()
 
 
 def taps_transform_kernel(taps_ref, forward_ref, out_ref, spread):
@@ -132,10 +155,10 @@
     if shown is not None:
         first_inv[0:EDGE, :] = first_inv[0:EDGE, :] * shown
     square[...] = jnp.zeros_like(square)
-    scaled[0:PAD, :] = jnp.zeros((PAD, LANES), F32)
-    product[0:PAD, :] = jnp.zeros((PAD, LANES), F32)
-
-    def one_tile(j, carry):
+    scaled[:, 0:PAD, :] = jnp.zeros((scaled.shape[0], PAD, LANES), F32)
+    product[:, 0:PAD, :] = jnp.zeros((scaled.shape[0], PAD, LANES), F32)
+
+    def one_tile(j, scaled, product):
         lanes = lanes_of(j)
         taps = tap_rows(gain_ref[0, 0:1, lanes], feat_ref, lanes)
         filter_taps = [se_ref[0, i : i + 1, lanes] for i in range(7)]
@@ -149,13 +172,18 @@
         for at in range(first_row, rows, STEP):
             q = three_taps(scaled, PAD + at, taps[0])
             f = se_filter(product, PAD + at, filter_taps)
-            result = (read(at, j) + q * f).astype(BF16)
-            mid_ref[at - first_row : at - first_row + STEP, lanes] = result
-            wide_result = result.astype(F32)
-            square[at : at + STEP, :] += wide_result * wide_result
+            result = read(at, j) + q * f
+            mid_ref[at - first_row : at - first_row + STEP, lanes] = result.astype(BF16)
+            square[at : at + STEP, :] += result * result
+
+    slots = scaled.shape[0]
+
+    def some_tiles(j, carry):
+        for i in range(slots):
+            one_tile(j * slots + i, scaled.at[i], product.at[i])
         return carry
 
-    lax.fori_loop(0, tiles, one_tile, 0)
+    lax.fori_loop(0, tiles // slots, some_tiles, 0)
     second = lax.rsqrt(
         jnp.sum(square[first_row:, :], axis=1, keepdims=True) / width + EPS
     )
@@ -168,7 +196,7 @@
 ):
     rows, width = tokens_ref.shape
     tail_refs, scratch = rest[: len(LATE)], rest[len(LATE) :]
-    scaled = scratch[2]
+    scaled = scratch[2].at[0]
 
     def read(at, j):
         return tokens_ref[at : at + STEP, lanes_of(j)].astype(F32)
@@ -202,10 +230,10 @@
     top = lax.broadcasted_iota(jnp.int32, (STEP, WIDE), 0) == 0
     for i, norms in enumerate((first[EDGE:], second)):
         left = to_row(norms, WIDE)
-        for k in range(3):
+        for k in range(PIECES):
             piece = left.astype(BF16).astype(F32)
             left = left - piece
-            lanes = pl.ds((i * 3 + k) * WIDE, WIDE)
+            lanes = pl.ds((i * PIECES + k) * WIDE, WIDE)
             rest_of = tail_refs[0][0:STEP, lanes].astype(F32)
             tail_refs[0][0:STEP, lanes] = jnp.where(top, piece, rest_of).astype(BF16)
 
@@ -219,13 +247,13 @@
     shown = jnp.where(first_block(), 0.0, 1.0)
 
     span = EARLY[1] // LANES
-    parts = EARLY[0] // EARLY[1]
+    own_part = EARLY[0] // LANES
 
     def read(at, j):
         if at < EDGE:
             part = lax.div(j, span)
-            row = jnp.where(part < parts, HALO + EDGE * part, HALO - EDGE)
-            column = j - span * part
+            row = jnp.where(j < own_part, HALO + EDGE * part, HALO - EDGE)
+            column = jnp.where(j < own_part, j - span * part, j - own_part)
             rows = pl.ds(pl.multiple_of(row + at, STEP), STEP)
             return early_ref[rows, lanes_of(column)].astype(F32)
         return tokens_ref[at - EDGE : at - EDGE + STEP, lanes_of(j)].astype(F32)
@@ -341,8 +369,8 @@
         shown = jnp.where(first_block(), 0.0, 1.0)
         for i, inverse in enumerate((first_inv, second_inv)):
             row = jnp.zeros((1, WIDE), F32)
-            for k in range(3):
-                lanes = pl.ds((i * 3 + k) * WIDE, WIDE)
+            for k in range(PIECES):
+                lanes = pl.ds((i * PIECES + k) * WIDE, WIDE)
                 row = row + stat_ref[0:STEP, lanes].astype(F32)[0:1]
             column = to_column(row * shown, start, HALO)
             inverse[...] = jnp.broadcast_to(column, inverse.shape)
@@ -399,44 +427,37 @@
     multiply_spectra(seen, table_ref, spectrum, lanes)
 
 
-def halo_results(tile, spectrum, backward_ref, base_ref, gate_ref, out_ref):
+def halo_results(
+    tile, spectrum, backward_ref, base_ref, gate_ref, out_ref, shown=None
+):
     lanes = pl.ds(tile * WIDE, WIDE)
     carried = jnp.dot(
         backward_ref[REACH:, :], spectrum[:, lanes], preferred_element_type=F32
     )
     for at in range(0, REACH, STEP):
+        gate = gate_ref[at : at + STEP, lanes]
+        if shown is not None:
+            gate = gate * shown
         out_ref[at : at + STEP, lanes] = (
-            base_ref[at : at + STEP, lanes]
-            + gate_ref[at : at + STEP, lanes] * carried[at : at + STEP]
+            base_ref[at : at + STEP, lanes] + gate * carried[at : at + STEP]
         ).astype(BF16)
 
 
 def tail_kernel(
-    tail_ref, shown_table_ref, forward_ref, backward_ref, base_ref, gate_ref, held_ref,
+    tail_ref, table_ref, forward_ref, backward_ref, base_ref, gate_ref, held_ref,
     out_ref,
-    product, spectrum,
+    spectrum,
 ):
     del held_ref
     shown = jnp.where(first_block(), 0.0, 1.0)
-    block = tail_ref.shape[1]
-
-    def arrived(tile):
-        lanes = pl.ds(tile * WIDE, WIDE)
-        for at in range(0, REACH, STEP):
-            w = tail_ref[at : at + STEP, lanes].astype(F32) * shown
-            if at == 0:
-                w = jnp.where(
-                    lax.broadcasted_iota(jnp.int32, w.shape, 0) == 0, 0.0, w
-                )
-            product[at : at + STEP, lanes] = w.astype(BF16)
 
     def spectra(tile):
-        halo_spectra(tile, product, forward_ref, shown_table_ref, spectrum)
+        halo_spectra(tile, tail_ref, forward_ref, table_ref, spectrum)
 
     def results(tile):
-        halo_results(tile, spectrum, backward_ref, base_ref, gate_ref, out_ref)
-
-    staggered(block // WIDE, arrived, spectra, results)
+        halo_results(tile, spectrum, backward_ref, base_ref, gate_ref, out_ref, shown)
+
+    staggered(tail_ref.shape[1] // WIDE, spectra, results)
 
 
 def whole(array):
@@ -446,21 +467,46 @@
 def on_device(tokens, norm_gain, feat_taps, se_taps, mr_taps):
     rows, width = tokens.shape
     total = rows + EDGE
-    forward, backward = transform_tables()
+    forward, backward, late_forward = transform_tables()
     length = lax.axis_size(("section", "ctx"))
 
     def from_behind(x):
         pairs = [(i, (i + 1) % length) for i in range(length)]
         return lax.ppermute(x, ("section", "ctx"), pairs)
 
-    start, size = EARLY
-    early = from_behind(
-        jnp.concatenate(
-            [tokens[rows - HALO :, start:]]
-            + [tokens[rows - EDGE :, i : i + size] for i in range(0, start, size)],
-            axis=0,
-        )
-    )
+    def place(i):
+        return i // RING, i % RING
+
+    def backward_hop(x):
+        pairs = []
+        for i in range(length):
+            line, z = place(i)
+            pairs.append((i, line * RING + (z - 1) % RING))
+        return lax.ppermute(x, ("section", "ctx"), pairs)
+
+    def last_hop(x):
+        pairs = []
+        for i in range(length):
+            line, z = place(i)
+            pairs.append((line * RING + (z - 2) % RING, (i + 1) % length))
+        return lax.ppermute(x, ("section", "ctx"), pairs)
+
+    parts = EARLY[0] // EARLY[1]
+    early, around = pl.pallas_call(
+        gather_kernel,
+        in_specs=[pl.BlockSpec(memory_space=pl.ANY)],
+        out_specs=[pl.BlockSpec(memory_space=pl.ANY)] * 2,
+        out_shape=[
+            jax.ShapeDtypeStruct((HALO + EDGE * parts, EARLY[1]), BF16),
+            jax.ShapeDtypeStruct((HALO, ROUND[1]), BF16),
+        ],
+        scratch_shapes=[pltpu.SemaphoreType.DMA((2 + parts,))],
+        compiler_params=params(),
+        cost_estimate=cost(1),
+        name="gather",
+    )(tokens)
+    around = backward_hop(around)
+    early = from_behind(early)
 
     groups = 2048 // 16
     table = pl.pallas_call(
@@ -484,12 +530,12 @@
         whole(se_taps),
     ]
 
-    def se_scratch(height):
+    def se_scratch(height, slots):
         return [
             pltpu.VMEM((height, LANES), F32),
             pltpu.VMEM((height, LANES), F32),
-            pltpu.VMEM((PAD + height, LANES), F32),
-            pltpu.VMEM((PAD + height, LANES), F32),
+            pltpu.VMEM((slots, PAD + height, LANES), F32),
+            pltpu.VMEM((slots, PAD + height, LANES), F32),
         ]
 
     def all_of(*shape):
@@ -511,12 +557,14 @@
             jax.ShapeDtypeStruct((mid_rows, LANES), F32),
         ]
         + [jax.ShapeDtypeStruct((REACH, size), BF16) for _, size in LATE],
-        scratch_shapes=se_scratch(rows),
+        scratch_shapes=se_scratch(rows, 1),
         compiler_params=params(),
         cost_estimate=cost(14),
         name="own_se",
     )(tokens, norm_gain, feat_taps, se_taps, feat_taps)
-    tails = [from_behind(tail) for tail in tails]
+    tails[0] = from_behind(tails[0])
+    around, mid = lax.optimization_barrier((around, mid))
+    around = backward_hop(around)
 
     head, head_inv = pl.pallas_call(
         head_se_kernel,
@@ -527,11 +575,16 @@
             jax.ShapeDtypeStruct((HEAD, width), BF16),
             jax.ShapeDtypeStruct((HEAD, LANES), F32),
         ],
-        scratch_shapes=se_scratch(HEAD),
+        scratch_shapes=se_scratch(HEAD, 4),
         compiler_params=params(),
         cost_estimate=cost(3),
         name="head_se",
     )(tokens, early, norm_gain, feat_taps, se_taps)
+
+    head, table, *later = lax.optimization_barrier((head, table, *tails[1:]))
+    tails[1:] = [from_behind(tail) for tail in later]
+    around, head = lax.optimization_barrier((around, head))
+    around = last_hop(around)
 
     def feat_spec(block, which, first):
         return pl.BlockSpec((1, 1, 3, 3, block), lambda j: (0, which, 0, 0, first + j))
@@ -577,53 +630,54 @@
     )(head, mid, head_inv, inv, norm_gain, feat_taps, table, forward, backward)
 
     block = HALO_BLOCK
-    first = start // block
-    out = pl.pallas_call(
-        functools.partial(halo_kernel, start=mid_rows - HALO),
-        grid=(size // block,),
-        in_specs=[
-            columns(HALO, block),
-            all_of(STEP, 6 * WIDE),
-            pl.BlockSpec((1, 2, block), lambda j: (0, 0, first + j)),
-            feat_spec(block, 0, first),
-            pl.BlockSpec((1, 7, block), lambda j: (0, 0, first + j)),
-            feat_spec(block, 1, first),
-            columns(POINTS, block, first),
-            whole(forward),
-            whole(backward),
-            columns(REACH, block, first),
-            columns(REACH, block, first),
-            pl.BlockSpec(memory_space=pl.ANY),
-        ],
-        out_specs=columns(REACH, block, first),
-        out_shape=jax.ShapeDtypeStruct((rows, width), BF16),
-        input_output_aliases={11: 0},
-        scratch_shapes=[
-            pltpu.VMEM((HALO, LANES), F32),
-            pltpu.VMEM((HALO, LANES), F32),
-            pltpu.VMEM((block // LANES, PAD + HALO, LANES), F32),
-            pltpu.VMEM((block // LANES, PAD + HALO, LANES), F32),
-            pltpu.VMEM((block // LANES, HALO, LANES), F32),
-            pltpu.VMEM((REACH, block), BF16),
-            pltpu.VMEM((POINTS, block), BF16),
-        ],
-        compiler_params=params(),
-        cost_estimate=cost(6),
-        name="halo",
-    )(
-        early, tails[0], norm_gain, feat_taps, se_taps, feat_taps, table,
-        forward, backward, base, gate, out,
-    )
-
-    block = TAIL_BLOCK
+    for (start, size), main in ((EARLY, early), (ROUND, around)):
+        first = start // block
+        out = pl.pallas_call(
+            functools.partial(halo_kernel, start=mid_rows - HALO),
+            grid=(size // block,),
+            in_specs=[
+                columns(HALO, block),
+                all_of(STEP, 2 * PIECES * WIDE),
+                pl.BlockSpec((1, 2, block), lambda j: (0, 0, first + j)),
+                feat_spec(block, 0, first),
+                pl.BlockSpec((1, 7, block), lambda j: (0, 0, first + j)),
+                feat_spec(block, 1, first),
+                columns(POINTS, block, first),
+                whole(forward),
+                whole(backward),
+                columns(REACH, block, first),
+                columns(REACH, block, first),
+                pl.BlockSpec(memory_space=pl.ANY),
+            ],
+            out_specs=columns(REACH, block, first),
+            out_shape=jax.ShapeDtypeStruct((rows, width), BF16),
+            input_output_aliases={11: 0},
+            scratch_shapes=[
+                pltpu.VMEM((HALO, LANES), F32),
+                pltpu.VMEM((HALO, LANES), F32),
+                pltpu.VMEM((block // LANES, PAD + HALO, LANES), F32),
+                pltpu.VMEM((block // LANES, PAD + HALO, LANES), F32),
+                pltpu.VMEM((block // LANES, HALO, LANES), F32),
+                pltpu.VMEM((REACH, block), BF16),
+                pltpu.VMEM((POINTS, block), BF16),
+            ],
+            compiler_params=params(),
+            cost_estimate=cost(6),
+            name="halo",
+        )(
+            main, tails[0], norm_gain, feat_taps, se_taps, feat_taps, table,
+            forward, backward, base, gate, out,
+        )
+
     for (start, size), tail in zip(LATE, tails):
+        block = TAIL_BLOCK
         out = pl.pallas_call(
             tail_kernel,
             grid=(size // block,),
             in_specs=[
                 columns(REACH, block),
                 columns(POINTS, block, start // block),
-                whole(forward),
+                whole(late_forward),
                 whole(backward),
                 columns(REACH, block, start // block),
                 columns(REACH, block, start // block),
@@ -633,13 +687,12 @@
             out_shape=jax.ShapeDtypeStruct((rows, width), BF16),
             input_output_aliases={6: 0},
             scratch_shapes=[
-                pltpu.VMEM((REACH, block), BF16),
                 pltpu.VMEM((POINTS, block), BF16),
             ],
             compiler_params=params(),
             cost_estimate=cost(3),
         name="tail",
-        )(tail, table, forward, backward, base, gate, out)
+        )(tail, table, late_forward, backward, base, gate, out)
     return out
 
 

time: 64.3 us -> 64.2 us (level)
  the two profiles are of different devices: /device:TPU:1 before, /device:TPU:7 now
where the time goes in v3:
time: 64.2 us; the launch traced here: 63.2 us
  Pallas kernels  43.8 us (68%)
  starting transfers between devices  9.3 us (14%)
  waiting for transfers between devices  7.47 us (12%)
  local copies, waits for them, and re-layouts  2.48 us (4%)
    pallas_call x1, Pallas kernels, on_device(): pl.pallas_call(own_se_kernel, grid=(1,), in_specs=[whole(tokens), *se_spe...  12.6 us
    pallas_call x1, Pallas kernels, on_device(): pl.pallas_call(own_mr_kernel, grid=(width // block,), in_specs=[columns(H...  12.2 us
    ppermute x4, waiting for transfers between devices, from_behind(): return lax.ppermute(x, ('section', 'ctx'), pairs)  7.46 us
    pallas_call x3, Pallas kernels, on_device(): pl.pallas_call(tail_kernel, grid=(size // block,), in_specs=[columns(REAC...  7.25 us
    pallas_call x2, Pallas kernels, on_device(): pl.pallas_call(functools.partial(halo_kernel, start=mid_rows - HALO), gri...  6.22 us
    ppermute x2, starting transfers between devices, backward_hop(): return lax.ppermute(x, ('section', 'ctx'), pairs)  3.65 us
    ppermute x1, starting transfers between devices, last_hop(): return lax.ppermute(x, ('section', 'ctx'), pairs)  2.88 us
    ppermute x4, starting transfers between devices, from_behind(): return lax.ppermute(x, ('section', 'ctx'), pairs)  2.76 us
  transfers between devices with their start and end apart: 7, of which 2 were waited for; matrix products, arithmetic and copies ran while one was open for 1% of the time, Pallas kernels for 65%

profile of v3, /device:TPU:7, one launch (start us, length us, event | category | flops | bytes accessed | tf_op | source)
XLA Modules:
  0.0 63.2 jit_solution(12486216581509152389)
XLA Ops:
  0.0 1.9 %copy-done = bf16[192,8192]{1,0:T(8,128)(2,1)S(1)} copy-done((bf16[192,8192]{1,0:T(8,128)(2,1)S(1)}, bf16[192,8192]{1,0:T(8,128)(2,1)}, u32[]{:S(2)}) %copy-start) | copy-done | bytes 3145752
  1.9 0.3 gather.1
  2.2 1.7 %collective-permute-start = (bf16[256,1024]{1,0:T(8,128)(2,1)S(1)}, bf16[256,1024]{1,0:T(8,128)(2,1)S(1)}, u32[]{:S(2)}, u32[]{:S(2)}) collective-permute-start(bf16[256,1024]{1,0:T(8,128)(2,1)S(1)} %get-tuple-element.25), channel_id=1, source_target_pairs={{0,1},{1,2},{2,3},{3,4},{4,5},{5,6},{6,7},{7,8},{8,9},{9,10},{10,1... | collective-permute-start | bytes 1572872 | tf_op jit(solution)/shard_map/ppermute | solution.py:475
  3.9 2.2 %collective-permute-start.2 = (bf16[144,1024]{1,0:T(8,128)(2,1)S(1)}, bf16[144,1024]{1,0:T(8,128)(2,1)S(1)}, u32[]{:S(2)}, u32[]{:S(2)}) collective-permute-start(bf16[144,1024]{1,0:T(8,128)(2,1)S(1)} %get-tuple-element.31), channel_id=1, source_target_pairs={{0,3},{1,0},{2,1},{3,2},{4,7},{5,4},{6,5},{7,6},{8,11},{9,8},{10,9... | collective-permute-start | bytes 884744 | tf_op jit(solution)/shard_map/ppermute | solution.py:485
  6.1 0.1 copy.15.se_ref
  6.2 0.0 copy-start.3
  6.3 0.4 copy.14.feat_ref.late_feat_ref.feat_first_ref
  6.7 12.6 %own_se.1 = (bf16[176,8192]{1,0:T(8,128)(2,1)S(1)}, f32[176,128]{1,0:T(8,128)S(1)}, bf16[128,2048]{1,0:T(8,128)(2,1)S(1)}, bf16[128,2048]{1,0:T(8,128)(2,1)S(1)}, bf16[128,2048]{1,0:T(8,128)(2,1)S(1)}) custom-call(bf16[192,8192]{1,0:T(8,128)(2,1)S(1)} %copy-done, f32[1,2,8192]{2,1,0:T(2,128)S(1)} %copy-done.4, ...), custom_call_target="tpu_custom_call" | custom-call | flops 14000000 | bytes 51800000 | tf_op jit(solution)/shard_map/own_se/pallas_call | solution.py:545
  19.3 1.5 %collective-permute-start.3 = (bf16[144,1024]{1,0:T(8,128)(2,1)S(1)}, bf16[144,1024]{1,0:T(8,128)(2,1)S(1)}, u32[]{:S(2)}, u32[]{:S(2)}) collective-permute-start(bf16[144,1024]{1,0:T(8,128)(2,1)S(1)} %collective-permute-done.2), channel_id=1, source_target_pairs={{0,3},{1,0},{2,1},{3,2},{4,7},{5,4},{6,5},{7,6},{8,11},{9,8},{10,9... | collective-permute-start | bytes 884744 | tf_op jit(solution)/shard_map/ppermute | solution.py:485
  20.8 0.1 collective-permute-start.5
  20.9 2.7 %taps_transform.1.table_ref = bf16[256,8192]{1,0:T(8,128)(2,1)S(1)} custom-call(bf16[128,512]{1,0:T(8,128)(2,1)S(1)} %bitcast.1, bf16[256,256]{1,0:T(8,128)(2,1)S(1)} %copy-done.3), custom_call_target="tpu_custom_call" | custom-call | flops 2500000 | bytes 9250000 | tf_op jit(solution)/shard_map/taps_transform/pallas_call | solution.py:512
  23.5 0.0 copy-start.2
  23.6 2.7 %head_se.1 = (bf16[32,8192]{1,0:T(8,128)(2,1)S(1)}, f32[32,128]{1,0:T(8,128)S(1)}) custom-call(bf16[192,8192]{1,0:T(8,128)(2,1)S(1)} %copy-done.1, bf16[256,1024]{1,0:T(8,128)(2,1)S(1)} %collective-permute-done.early_ref.main_ref, f32[1,2,8192]{2,1,0:T(2,128)S(1)} %copy-done.4, f32[1,2,3,3,8192]{4,3,2,1,0:T(4,128)S(1)} %copy.14.feat_ref.late_feat_ref.feat_first_ref, ...), custom_call_target="tpu_custom_call" | custom-call | flops 3000000 | bytes 11100000 | tf_op jit(solution)/shard_map/head_se/pallas_call | solution.py:569
  26.2 0.1 collective-permute-start.4
  26.3 0.9 %collective-permute-start.1 = (bf16[128,2048]{1,0:T(8,128)(2,1)S(1)}, bf16[128,2048]{1,0:T(8,128)(2,1)S(1)}, u32[]{:S(2)}, u32[]{:S(2)}) collective-permute-start(bf16[128,2048]{1,0:T(8,128)(2,1)S(1)} %get-tuple-element.29), channel_id=1, source_target_pairs={{0,1},{1,2},{2,3},{3,4},{4,5},{5,6},{6,7},{7,8},{8,9},{9,10},{10,1... | collective-permute-start | bytes 1572872 | tf_op jit(solution)/shard_map/ppermute | solution.py:475
  27.2 2.9 %collective-permute-start.6 = (bf16[144,1024]{1,0:T(8,128)(2,1)S(1)}, bf16[144,1024]{1,0:T(8,128)(2,1)S(1)}, u32[]{:S(2)}, u32[]{:S(2)}) collective-permute-start(bf16[144,1024]{1,0:T(8,128)(2,1)S(1)} %collective-permute-done.3), channel_id=1, source_target_pairs={{2,1},{3,2},{0,3},{1,4},{6,5},{7,6},{4,7},{5,8},{10,9},{11,10},{8,... | collective-permute-start | bytes 884744 | tf_op jit(solution)/shard_map/ppermute | solution.py:492
  30.1 12.2 %own_mr.1 = (bf16[192,8192]{1,0:T(8,128)(2,1)}, f32[128,8192]{1,0:T(8,128)S(1)}, f32[128,8192]{1,0:T(8,128)S(1)}) custom-call(bf16[32,8192]{1,0:T(8,128)(2,1)S(1)} %get-tuple-element.35.head_ref, bf16[176,8192]{1,0:T(8,128)(2,1)S(1)} %get-tuple-element.36.mid_ref, f32[32,128]{1,0:T(8,128)S(1)} %get-tuple-element.37.head_inv_ref, ...), custom_call_target="tpu_custom_call" | custom-call | flops 12000000 | bytes 44400000 | tf_op jit(solution)/shard_map/own_mr/pallas_call | solution.py:596
  42.3 7.3 %collective-permute-done.5.stat_ref.tail_ref = bf16[128,2048]{1,0:T(8,128)(2,1)S(1)} collective-permute-done((bf16[128,2048]{1,0:T(8,128)(2,1)S(1)}, bf16[128,2048]{1,0:T(8,128)(2,1)S(1)}, u32[]{:S(2)}, u32[]{:S(2)}) %collective-permute-start.5) | collective-permute-done | bytes 524320 | tf_op jit(solution)/shard_map/ppermute | solution.py:475
  49.6 3.1 %halo.2.held_ref = bf16[192,8192]{1,0:T(8,128)(2,1)} custom-call(bf16[256,1024]{1,0:T(8,128)(2,1)S(1)} %collective-permute-done.early_ref.main_ref, bf16[128,2048]{1,0:T(8,128)(2,1)S(1)} %collective-permute-done.5.stat_ref.tail_ref, f32[1,2,8192]{2,1,0:T(2,128)S(1)} %copy-done.4, ...), custom_call_target="tpu_custom_call", output_to_operand_aliasing={{}: (11, {})} | custom-call | flops 6000000 | bytes 22200000 | tf_op jit(solution)/shard_map/halo/pallas_call | solution.py:635
  52.7 3.1 %halo.3.held_ref = bf16[192,8192]{1,0:T(8,128)(2,1)} custom-call(bf16[144,1024]{1,0:T(8,128)(2,1)S(1)} %collective-permute-done.6.main_ref, bf16[128,2048]{1,0:T(8,128)(2,1)S(1)} %collective-permute-done.5.stat_ref.tail_ref, f32[1,2,8192]{2,1,0:T(2,128)S(1)} %copy-done.4, ...), custom_call_target="tpu_custom_call", output_to_operand_aliasing={{}: (11, {})} | custom-call | flops 6000000 | bytes 22200000 | tf_op jit(solution)/shard_map/halo/pallas_call | solution.py:635
  55.8 2.4 %tail.3.held_ref = bf16[192,8192]{1,0:T(8,128)(2,1)} custom-call(bf16[128,2048]{1,0:T(8,128)(2,1)S(1)} %collective-permute-done.5.stat_ref.tail_ref, bf16[256,8192]{1,0:T(8,128)(2,1)S(1)} %taps_transform.1.table_ref, bf16[256,128]{1,0:T(8,128)(2,1)S(1)} %copy-done.5, bf16[256,256]{1,0:T(8,128)(2,1)S(1)} %copy-done.2, ...), custom_call_target="tpu_custom_call", output_to_operand_aliasing={{}: (6, {})} | custom-call | flops 3000000 | bytes 11100000 | tf_op jit(solution)/shard_map/tail/pallas_call | solution.py:674
  58.2 2.4 %tail.4.held_ref = bf16[192,8192]{1,0:T(8,128)(2,1)} custom-call(bf16[128,2048]{1,0:T(8,128)(2,1)S(1)} %collective-permute-done.4.tail_ref, bf16[256,8192]{1,0:T(8,128)(2,1)S(1)} %taps_transform.1.table_ref, bf16[256,128]{1,0:T(8,128)(2,1)S(1)} %copy-done.5, bf16[256,256]{1,0:T(8,128)(2,1)S(1)} %copy-done.2, ...), custom_call_target="tpu_custom_call", output_to_operand_aliasing={{}: (6, {})} | custom-call | flops 3000000 | bytes 11100000 | tf_op jit(solution)/shard_map/tail/pallas_call | solution.py:674
  60.6 0.2 collective-permute-done.1.tail_ref
  60.8 2.4 %tail.5 = bf16[192,8192]{1,0:T(8,128)(2,1)} custom-call(bf16[128,2048]{1,0:T(8,128)(2,1)S(1)} %collective-permute-done.1.tail_ref, bf16[256,8192]{1,0:T(8,128)(2,1)S(1)} %taps_transform.1.table_ref, bf16[256,128]{1,0:T(8,128)(2,1)S(1)} %copy-done.5, bf16[256,256]{1,0:T(8,128)(2,1)S(1)} %copy-done.2, ...), custom_call_target="tpu_custom_call", output_to_operand_aliasing={{}: (6, {})} | custom-call | flops 3000000 | bytes 11100000 | tf_op jit(solution)/shard_map/tail/pallas_call | solution.py:674
  (20 shorter events, 0.0 us)
Async XLA Ops:
  0.0 1.9 %copy-start = (bf16[192,8192]{1,0:T(8,128)(2,1)S(1)}, bf16[192,8192]{1,0:T(8,128)(2,1)}, u32[]{:S(2)}) copy-start(bf16[192,8192]{1,0:T(8,128)(2,1)} %tokens_ref.5) | copy-start | bytes 9437188
  1.9 4.2 %copy-start.8 = (f32[1,7,8192]{2,0,1:T(1,128)S(1)}, f32[1,7,8192]{2,0,1:T(1,128)}, u32[]{:S(2)}) copy-start(f32[1,7,8192]{2,0,1:T(1,128)} %param.11) | copy-start | bytes 688132
  1.9 4.3 %copy-start.7 = (f32[1,2,3,3,8192]{4,1,3,2,0:T(2,128)S(1)}, f32[1,2,3,3,8192]{4,1,3,2,0:T(2,128)}, u32[]{:S(2)}) copy-start(f32[1,2,3,3,8192]{4,1,3,2,0:T(2,128)} %param.10) | copy-start | bytes 1769476
  1.9 4.8 %copy-start.4 = (f32[1,2,8192]{2,1,0:T(2,128)S(1)}, f32[1,2,8192]{2,1,0:T(2,128)}, u32[]{:S(2)}) copy-start(f32[1,2,8192]{2,1,0:T(2,128)} %gain_ref.9) | copy-start | bytes 196612
  2.2 21.4 %collective-permute-start = (bf16[256,1024]{1,0:T(8,128)(2,1)S(1)}, bf16[256,1024]{1,0:T(8,128)(2,1)S(1)}, u32[]{:S(2)}, u32[]{:S(2)}) collective-permute-start(bf16[256,1024]{1,0:T(8,128)(2,1)S(1)} %get-tuple-element.25), channel_id=1, source_target_pairs={{0,1},{1,2},{2,3},{3,4},{4,5},{5,6},{6,7},{7,8},{8,9},{9,10},{10,1... | collective-permute-start | bytes 1572872 | tf_op jit(solution)/shard_map/ppermute | solution.py:475
  3.9 15.4 %collective-permute-start.2 = (bf16[144,1024]{1,0:T(8,128)(2,1)S(1)}, bf16[144,1024]{1,0:T(8,128)(2,1)S(1)}, u32[]{:S(2)}, u32[]{:S(2)}) collective-permute-start(bf16[144,1024]{1,0:T(8,128)(2,1)S(1)} %get-tuple-element.31), channel_id=1, source_target_pairs={{0,3},{1,0},{2,1},{3,2},{4,7},{5,4},{6,5},{7,6},{8,11},{9,8},{10,9... | collective-permute-start | bytes 884744 | tf_op jit(solution)/shard_map/ppermute | solution.py:485
  6.2 14.6 %copy-start.3 = (bf16[256,256]{1,0:T(8,128)(2,1)S(1)}, bf16[256,256]{1,0:T(8,128)(2,1)}, u32[]{:S(2)}) copy-start(bf16[256,256]{1,0:T(8,128)(2,1)} %constant.6.clone.forward_ref) | copy-start | bytes 393220
  6.3 14.6 %copy-start.6 = (bf16[1,128,512]{2,1,0:T(8,128)(2,1)S(1)}, bf16[1,128,512]{2,1,0:T(8,128)(2,1)}, u32[]{:S(2)}) copy-start(bf16[1,128,512]{2,1,0:T(8,128)(2,1)} %param.12) | copy-start | bytes 393220
  19.3 4.3 %copy-start.1 = (bf16[192,8192]{1,0:T(8,128)(2,1)S(1)}, bf16[192,8192]{1,0:T(8,128)(2,1)}, u32[]{:S(2)}) copy-start(bf16[192,8192]{1,0:T(8,128)(2,1)} %tokens_ref.5) | copy-start | bytes 9437188
  19.3 7.9 %collective-permute-start.3 = (bf16[144,1024]{1,0:T(8,128)(2,1)S(1)}, bf16[144,1024]{1,0:T(8,128)(2,1)S(1)}, u32[]{:S(2)}, u32[]{:S(2)}) collective-permute-start(bf16[144,1024]{1,0:T(8,128)(2,1)S(1)} %collective-permute-done.2), channel_id=1, source_target_pairs={{0,3},{1,0},{2,1},{3,2},{4,7},{5,4},{6,5},{7,6},{8,11},{9,8},{10,9... | collective-permute-start | bytes 884744 | tf_op jit(solution)/shard_map/ppermute | solution.py:485
  20.8 28.8 %collective-permute-start.5 = (bf16[128,2048]{1,0:T(8,128)(2,1)S(1)}, bf16[128,2048]{1,0:T(8,128)(2,1)S(1)}, u32[]{:S(2)}, u32[]{:S(2)}) collective-permute-start(bf16[128,2048]{1,0:T(8,128)(2,1)S(1)} %get-tuple-element.42), channel_id=1, source_target_pairs={{0,1},{1,2},{2,3},{3,4},{4,5},{5,6},{6,7},{7,8},{8,9},{9,10},{10,1... | collective-permute-start | bytes 1572872 | tf_op jit(solution)/shard_map/ppermute | solution.py:475
  23.5 6.6 %copy-start.2 = (bf16[256,256]{1,0:T(8,128)(2,1)S(1)}, bf16[256,256]{1,0:T(8,128)(2,1)}, u32[]{:S(2)}) copy-start(bf16[256,256]{1,0:T(8,128)(2,1)} %constant.7.clone.backward_ref) | copy-start | bytes 393220
  26.2 32.0 %collective-permute-start.4 = (bf16[128,2048]{1,0:T(8,128)(2,1)S(1)}, bf16[128,2048]{1,0:T(8,128)(2,1)S(1)}, u32[]{:S(2)}, u32[]{:S(2)}) collective-permute-start(bf16[128,2048]{1,0:T(8,128)(2,1)S(1)} %get-tuple-element.41), channel_id=1, source_target_pairs={{0,1},{1,2},{2,3},{3,4},{4,5},{5,6},{6,7},{7,8},{8,9},{9,10},{10,1... | collective-permute-start | bytes 1572872 | tf_op jit(solution)/shard_map/ppermute | solution.py:475
  26.3 34.5 %collective-permute-start.1 = (bf16[128,2048]{1,0:T(8,128)(2,1)S(1)}, bf16[128,2048]{1,0:T(8,128)(2,1)S(1)}, u32[]{:S(2)}, u32[]{:S(2)}) collective-permute-start(bf16[128,2048]{1,0:T(8,128)(2,1)S(1)} %get-tuple-element.29), channel_id=1, source_target_pairs={{0,1},{1,2},{2,3},{3,4},{4,5},{5,6},{6,7},{7,8},{8,9},{9,10},{10,1... | collective-permute-start | bytes 1572872 | tf_op jit(solution)/shard_map/ppermute | solution.py:475
  27.2 25.5 %collective-permute-start.6 = (bf16[144,1024]{1,0:T(8,128)(2,1)S(1)}, bf16[144,1024]{1,0:T(8,128)(2,1)S(1)}, u32[]{:S(2)}, u32[]{:S(2)}) collective-permute-start(bf16[144,1024]{1,0:T(8,128)(2,1)S(1)} %collective-permute-done.3), channel_id=1, source_target_pairs={{2,1},{3,2},{0,3},{1,4},{6,5},{7,6},{4,7},{5,8},{10,9},{11,10},{8,... | collective-permute-start | bytes 884744 | tf_op jit(solution)/shard_map/ppermute | solution.py:492
  52.7 3.1 %copy-start.5 = (bf16[256,128]{1,0:T(8,128)(2,1)S(1)}, bf16[256,128]{1,0:T(8,128)(2,1)}, u32[]{:S(2)}) copy-start(bf16[256,128]{1,0:T(8,128)(2,1)} %constant.8.clone.forward_ref) | copy-start | bytes 196612
